TPU v7x, 128 devices: a whole 4x4x4 slice. The times are simulated.
128 devices in a mesh: role: 2 (over y_hi), vocab: 64 (over x, y_lo, z, core).
Axes of the slice: x: 4, y: 4 (y_hi: 2, y_lo: 2; y = y_hi * 2 + y_lo), z: 4, core: 2. Of those that a mesh axis runs over, the one named last changes fastest.
Arguments:
- teacher_hidden: bfloat16 [256, 16384], P('role', 'vocab'), may hold values from -600 to 600
- teacher_gain: bfloat16 [16384], replicated, may hold values from 0.25 to 1.75
- teacher_head: bfloat16 [65536, 16384], P(('role', 'vocab')), may hold values from -0.3125 to 0.3125
- student_hidden: bfloat16 [256, 4096], P(('role', 'vocab')), may hold values from -600 to 600
- student_gain: bfloat16 [4096], replicated, may hold values from 0.25 to 1.75
- student_head: bfloat16 [65536, 4096], P(('role', 'vocab')), may hold values from -0.625 to 0.625
- token_ids: int32 [256], replicated, may hold values from 0 to 65535
- teacher_map: int32 [128], replicated, may hold values from 0 to 127, each once
- student_map: int32 [128], replicated, may hold values from 0 to 127, each once
Outputs:
- loss: float32 [], replicated
- head_grad: bfloat16 [65536, 4096], P(('role', 'vocab'))
- input_grad: float32 [256, 4096], P(('role', 'vocab'))
Inputs may be any that keep to these rules, and one draw needn't show every extreme that they name: A permutation: each of the 128 vocabulary blocks once; rows i * 512 to (i + 1) * 512 - 1 of teacher_head belong to vocabulary block teacher_map[i]. A permutation: each of the 128 vocabulary blocks once; rows i * 512 to (i + 1) * 512 - 1 of student_head belong to vocabulary block student_map[i].
All inputs are finite; a program needn't handle non-finite values.
Results may differ from a plain program's by a relative error of at most 0.0095.
The roundings to bfloat16 on the way count: a program that leaves them out, or rounds other values in their place, can miss the bound.
Values may be sent and summed in bfloat16 or wider, within the bound.
A program may use at most 128 MiB of HBM per device.

v0:
```python
import jax
import jax.numpy as jnp
from jax import lax
from jax.sharding import PartitionSpec as P

EPS = 1e-05
LOSS_SCALE = 256.0
CE_WEIGHT = 0.25


def normalize(rows, gain):
    rows_f = rows.astype(jnp.float32)
    scale = lax.rsqrt(jnp.mean(rows_f * rows_f, axis=-1, keepdims=True) + EPS)
    return (rows_f * scale * gain.astype(jnp.float32), scale)


def positions(mapping, wanted):
    count = mapping.shape[0]
    match = mapping[None, :] == wanted[:, None]
    return jnp.sum(jnp.where(match, jnp.arange(count, dtype=jnp.int32)[None, :], 0), axis=1)


def contract_rows(left, right):
    return lax.dot_general(
        left, right, (((1,), (1,)), ((), ())), preferred_element_type=jnp.float32
    )


def token_terms(teach_vals, stud_vals, label_hit):
    teach_top = jnp.max(teach_vals, axis=1, keepdims=True)
    teach_log = teach_top + jnp.log(jnp.sum(jnp.exp(teach_vals - teach_top), axis=1, keepdims=True))
    stud_top = jnp.max(stud_vals, axis=1, keepdims=True)
    stud_log = stud_top + jnp.log(jnp.sum(jnp.exp(stud_vals - stud_top), axis=1, keepdims=True))
    teach_prob = jnp.exp(teach_vals - teach_log)
    stud_prob = jnp.exp(stud_vals - stud_log)
    diverge = (
        jnp.sum(teach_prob * (teach_vals - stud_vals), axis=1) - teach_log[:, 0] + stud_log[:, 0]
    )
    picked = jnp.sum(jnp.where(label_hit, stud_vals, 0.0), axis=1)
    cross_ent = stud_log[:, 0] - picked
    hit_f = label_hit.astype(jnp.float32)
    grad = (LOSS_SCALE * ((1.0 + CE_WEIGHT) * stud_prob - teach_prob - CE_WEIGHT * hit_f)).astype(
        jnp.bfloat16
    )
    return (diverge + CE_WEIGHT * cross_ent, grad)


def body(
    teacher_hidden,
    teacher_gain,
    teacher_head,
    student_hidden,
    student_gain,
    student_head,
    token_ids,
    teacher_map,
    student_map,
):
    section = lax.all_gather(teacher_hidden, "role", axis=0, tiled=True)
    tokens_all = section.shape[0]
    width = teacher_head.shape[0]
    full_rows = lax.all_gather(section, "vocab", axis=1, tiled=True)
    normed = normalize(full_rows, teacher_gain)[0].astype(jnp.bfloat16)
    teach_sum = contract_rows(normed, teacher_head)
    teacher_logits = teach_sum.astype(jnp.bfloat16)
    student_all = lax.all_gather(student_hidden, ("role", "vocab"), axis=0, tiled=True)
    stud_norm, stud_scale = normalize(student_all, student_gain)
    student_normed = stud_norm.astype(jnp.bfloat16)
    student_logits = contract_rows(student_normed, student_head).astype(jnp.bfloat16)
    nblk = teacher_map.shape[0]
    order = positions(teacher_map, student_map)
    label_col = positions(student_map, token_ids // width) * width + token_ids % width
    device = lax.axis_index(("role", "vocab"))
    own_rows = student_hidden.shape[0]
    teach_tok, stud_tok = (
        lax.all_to_all(teacher_logits, ("role", "vocab"), split_axis=0, concat_axis=1, tiled=True),
        lax.all_to_all(student_logits, ("role", "vocab"), split_axis=0, concat_axis=1, tiled=True),
    )
    ordered = teach_tok.reshape(own_rows, nblk, width)[:, order, :].reshape(own_rows, nblk * width)
    own_cols = lax.dynamic_slice_in_dim(label_col, device * own_rows, own_rows)
    label_hit = jnp.arange(nblk * width, dtype=jnp.int32)[None, :] == own_cols[:, None]
    per_token, grad_tokens = token_terms(
        ordered.astype(jnp.float32), stud_tok.astype(jnp.float32), label_hit
    )
    loss = lax.psum(jnp.sum(per_token), ("role", "vocab")) / tokens_all
    grad = lax.all_to_all(grad_tokens, ("role", "vocab"), split_axis=1, concat_axis=0, tiled=True)
    head_grad = lax.dot_general(
        grad, student_normed, (((0,), (0,)), ((), ())), preferred_element_type=jnp.float32
    ).astype(jnp.bfloat16)
    hidden_back = lax.psum_scatter(
        jnp.dot(grad, student_head, preferred_element_type=jnp.float32),
        ("role", "vocab"),
        scatter_dimension=0,
        tiled=True,
    )
    own_scale = lax.dynamic_slice_in_dim(stud_scale, device * own_rows, own_rows, 0)
    hat = student_hidden.astype(jnp.float32) * own_scale
    back = hidden_back * student_gain.astype(jnp.float32)
    input_grad = own_scale * (back - hat * jnp.mean(back * hat, axis=1, keepdims=True))
    return (loss, head_grad, input_grad)


def solution(mesh):
    placed = (
        P("role", "vocab"),
        P(),
        P(("role", "vocab"), None),
        P(("role", "vocab"), None),
        P(),
        P(("role", "vocab"), None),
        P(),
        P(),
        P(),
    )
    return jax.shard_map(
        body,
        mesh=mesh,
        in_specs=placed,
        out_specs=(P(), P(("role", "vocab"), None), P(("role", "vocab"), None)),
        check_vma=False,
    )
```

profile of v0, /device:TPU:1, one launch (start us, length us, event | category | flops | bytes accessed | tf_op | source)
XLA Modules:
  0.0 558.5 jit_solution(2812259362403922991)
XLA Ops:
  7.2 0.0 all-gather.6.cloned.1.call-start
  7.2 0.7 all-gather.6.cloned.1.call-update
  7.9 0.0 all-gather.4.cloned.1.call-start
  7.9 7.8 %all_gather.9 = bf16[256,256]{1,0:T(8,128)(2,1)} all-gather(bf16[128,256]{1,0:T(8,128)(2,1)} %param.9), channel_id=1, replica_groups=mesh['role'=2,'vocab'=64] {'role'}, dimensions={0}, use_global_device_ids=true | all-gather | bytes 196608 | tf_op jit(solution)/shard_map/all_gather | solution.py:59
  15.8 0.0 all-gather.4.cloned.1.call-update
  15.8 0.7 convert_element_type.58
  16.5 0.8 convert_element_type.53
  17.3 0.8 select_reduce_fusion.1
  18.1 0.7 and_select_fusion.1
  18.8 0.8 select_reduce_fusion
  19.6 0.7 fusion.24
  20.3 186.7 %all-gather.6.cloned.1.call-done = bf16[128,2,4096]{2,1,0:T(2,128)(2,1)} async-done(((bf16[1,2,4096]{2,1,0:T(2,128)(2,1)}), bf16[128,2,4096]{2,1,0:T(2,128)(2,1)}) %all-gather.6.cloned.1.call-update) | async-done | bytes 2097168 | tf_op jit(solution)/shard_map/all_gather | solution.py:66
  207.0 4.5 reshape.151
  211.4 0.0 copy-start
  211.4 2.7 multiply_reduce_fusion
  214.1 0.7 copy-done
  214.9 3.6 convolution_convert_fusion.1
  218.5 0.8 all_to_all.37
  219.3 7.0 %all-to-all-start.1 = ((bf16[128,2,512]{2,1,0:T(2,128)(2,1)}), bf16[128,2,512]{2,1,0:T(2,128)(2,1)S(1)}, u32[]{:S(2)}, u32[]{:S(2)}) async-start(bf16[128,2,512]{2,1,0:T(2,128)(2,1)} %all_to_all.37), calls=%async_computation.1 | async-start | bytes 524288 | tf_op jit(solution)/shard_map/all_to_all | solution.py:77
  226.4 111.3 %all-gather.4.cloned.1.call-done = bf16[256,16384]{1,0:T(8,128)(2,1)} async-done(((bf16[256,256]{1,0:T(8,128)(2,1)}), bf16[256,16384]{1,0:T(8,128)(2,1)}) %all-gather.4.cloned.1.call-update) | async-done | bytes 8388624 | tf_op jit(solution)/shard_map/all_gather | solution.py:62
  337.7 5.1 fusion
  342.9 11.7 %fusion.7 = bf16[256,512]{1,0:T(8,128)(2,1)S(1)} fusion(bf16[512,16384]{1,0:T(8,128)(2,1)} %param.11, bf16[256,16384]{1,0:T(8,128)(2,1)} %all-gather.4.cloned.1.call-done, f32[16384]{0:T(1024)S(1)} %convert_element_type.53, f32[256]{0:T(256)S(1)} %add_rsqrt_fusion.1), kind=kOutput, calls=%fused_computation.13 | convolution fusion | flops 4311875584 | bytes 25494528 | tf_op jit(solution)/shard_map/dot_general | solution.py:24
  354.5 0.8 all_to_all.34
  355.3 0.0 all-to-all-done.1
  355.3 6.7 %all-to-all-start = ((bf16[128,2,512]{2,1,0:T(2,128)(2,1)}), bf16[128,2,512]{2,1,0:T(2,128)(2,1)S(1)}, u32[]{:S(2)}, u32[]{:S(2)}) async-start(bf16[128,2,512]{2,1,0:T(2,128)(2,1)} %all_to_all.34), calls=%async_computation | async-start | bytes 524288 | tf_op jit(solution)/shard_map/all_to_all | solution.py:76
  362.0 0.0 all-reduce.3.cloned.1.call-start
  362.1 0.1 dynamic_slice.4
  362.2 0.7 reduce_max.30
  362.9 10.6 %all-to-all-done = bf16[128,2,512]{2,1,0:T(2,128)(2,1)S(1)} async-done(((bf16[128,2,512]{2,1,0:T(2,128)(2,1)}), bf16[128,2,512]{2,1,0:T(2,128)(2,1)S(1)}, u32[]{:S(2)}, u32[]{:S(2)}) %all-to-all-start) | async-done | bytes 262176 | tf_op jit(solution)/shard_map/all_to_all | solution.py:76
  373.5 1.1 gather_fusion
  374.6 0.7 reduce_max.28
  375.3 0.3 fusion.22
  375.6 0.5 fusion.15
  376.0 0.6 add_reduce_fusion
  376.7 0.3 fusion.13
  377.0 0.3 copy.17
  377.3 15.1 %all_to_all.45 = bf16[2,128,512]{2,0,1:T(2,128)(2,1)S(1)} all-to-all(bf16[2,128,512]{2,0,1:T(2,128)(2,1)S(1)} %copy.17), channel_id=1, replica_groups=mesh['role'=2,'vocab'=64] {'role','vocab'}, dimensions={1} | all-to-all | bytes 524288 | tf_op jit(solution)/shard_map/all_to_all | solution.py:86
  392.4 0.1 all_to_all.41
  392.5 5.4 fusion.26
  397.9 0.0 all-reduce.3.cloned.1.call-update
  397.9 0.1 dynamic-slice.3
  398.0 62.6 %psum.7 = f32[]{:T(128)} all-reduce(f32[]{:T(128)} %get-tuple-element.6), channel_id=1, replica_groups=mesh['role'=2,'vocab'=64] {'role','vocab'}, use_global_device_ids=true, to_apply=%region_11.12 | all-reduce | flops 1 | bytes 8 | tf_op jit(solution)/shard_map/psum | solution.py:85
  461.3 0.0 copy-start.1
  461.3 5.6 %convolution_convert_fusion = bf16[512,4096]{1,0:T(8,128)(2,1)} fusion(bf16[256,512]{1,0:T(8,128)(2,1)S(1)} %all_to_all.41, f32[256,4096]{1,0:T(8,128)} %reshape.151, f32[4096]{0:T(1024)S(1)} %convert_element_type.58, f32[256]{0:T(256)S(1)} %add_rsqrt_fusion), kind=kOutput, calls=%fused_computation.9 | convolution fusion | flops 1078984704 | bytes 8668160 | tf_op jit(solution)/shard_map/dot_general | solution.py:87
  466.9 81.1 %all-reduce.3.cloned.1.call-done = f32[256,4096]{1,0:T(8,128)} async-done(((f32[256,4096]{1,0:T(8,128)}), f32[256,4096]{1,0:T(8,128)}) %all-reduce.3.cloned.1.call-update) | async-done | bytes 4194320
  548.1 0.0 copy-done.1
  548.1 1.1 multiply_reduce_fusion.1
  549.2 1.6 subtract_multiply_fusion
  (9 shorter events, 0.1 us)
Async XLA Ops:
  7.2 199.8 %all-gather.6.cloned.1.call-start = ((), (), s32[]{:S(2)}) async-start(), calls=%async_computation.4 | async-start | bytes 2113536 | tf_op jit(solution)/shard_map/all_gather | solution.py:66
  7.9 329.8 %all-gather.4.cloned.1.call-start = ((), (), s32[]{:S(2)}) async-start(), calls=%async_computation.3 | async-start | bytes 8519680 | tf_op jit(solution)/shard_map/all_gather | solution.py:62
  211.4 3.4 copy-start
  219.3 136.0 %all-to-all-start.1 = ((bf16[128,2,512]{2,1,0:T(2,128)(2,1)}), bf16[128,2,512]{2,1,0:T(2,128)(2,1)S(1)}, u32[]{:S(2)}, u32[]{:S(2)}) async-start(bf16[128,2,512]{2,1,0:T(2,128)(2,1)} %all_to_all.37), calls=%async_computation.1 | async-start | bytes 524288 | tf_op jit(solution)/shard_map/all_to_all | solution.py:77
  355.3 18.2 %all-to-all-start = ((bf16[128,2,512]{2,1,0:T(2,128)(2,1)}), bf16[128,2,512]{2,1,0:T(2,128)(2,1)S(1)}, u32[]{:S(2)}, u32[]{:S(2)}) async-start(bf16[128,2,512]{2,1,0:T(2,128)(2,1)} %all_to_all.34), calls=%async_computation | async-start | bytes 524288 | tf_op jit(solution)/shard_map/all_to_all | solution.py:76
  362.0 186.0 %all-reduce.3.cloned.1.call-start = ((), (), s32[]{:S(2)}) async-start(), calls=%async_computation.5 | async-start | bytes 8388608
  461.3 86.7 %copy-start.1 = (bf16[2,4096]{1,0:T(2,128)(2,1)S(1)}, bf16[2,4096]{1,0:T(2,128)(2,1)}, u32[]{:S(2)}) copy-start(bf16[2,4096]{1,0:T(2,128)(2,1)} %param.12) | copy-start | bytes 49156
Sparse Core Ops, SparseCore 0:
  9.7 197.2 all-gather.5
  208.6 129.0 all-gather.3
  398.1 149.9 all-reduce.2
where the time goes:
time: 559 us; the launch traced here: 558 us
  waiting for transfers between devices  390 us (70%)
  blocking collectives  85.6 us (15%)
  matrix products  26.3 us (5%)
  other arithmetic  18.2 us (3%)
  between operations  15.6 us (3%)
  starting transfers between devices  13.8 us (2%)
  local copies, waits for them, and re-layouts  8.47 us (2%)
    all_gather x1, waiting for transfers between devices, body(): lax.all_gather(student_hidden, ('role', 'vocab'), axis=0, tiled=True)  187 us
    all_gather x1, waiting for transfers between devices, body(): full_rows = lax.all_gather(section, 'vocab', axis=1, tiled=True)  111 us
    unnamed x4, waiting for transfers between devices  81.9 us
    psum x1, blocking collectives, body(): loss = lax.psum(jnp.sum(per_token), ('role', 'vocab')) / tokens_all  62.6 us
    dot_general x2, matrix products, contract_rows(): lax.dot_general(left, right, (((1,), (1,)), ((), ())), preferred_element_...  15.3 us
    all_to_all x1, blocking collectives, body(): lax.all_to_all(grad_tokens, ('role', 'vocab'), split_axis=1, concat_axis=...  15.1 us
  transfers between devices with their start and end apart: 5, of which 4 were waited for; matrix products, arithmetic and copies ran while one was open for 7% of the time, Pallas kernels for 0%

commit v1 on v0

v1 whole, which is shorter than its diff:
```python
import jax
import jax.numpy as jnp
from jax import lax
from jax.experimental import pallas as pl
from jax.experimental.pallas import tpu as pltpu
from jax.sharding import PartitionSpec as P

EPS = 1e-05
LOSS_SCALE = 256.0
CE_WEIGHT = 0.25
MESH = pl.DeviceIdType.MESH
F32 = jnp.float32
BF16 = jnp.bfloat16
X, Y, Z = 0, 1, 2
ALL = pl.ds(0, 4)
PARTS = (((Y, Z, X), 0, 32), ((Z, X, Y), 32, 48), ((X, Y, Z), 80, 48))
N_SEM = 232


def div(a, b):
    return lax.div(a, jnp.int32(b))


def rem(a, b):
    return lax.rem(a, jnp.int32(b))


def flat_of(x, y, z, c):
    return div(y, 2) * 64 + ((x * 2 + rem(y, 2)) * 4 + z) * 2 + c


def shuffle4(tiles, pair):
    out = []
    for b in range(4):
        acc = None
        for a in range(4):
            shift = (2 * (a - b)) % 8
            moved = pltpu.roll(tiles[a], shift, 0) if shift else tiles[a]
            acc = moved if acc is None else jnp.where(pair == a, moved, acc)
        out.append(acc)
    return out


def kernel(
    t_ref,
    tg_ref,
    th_hbm,
    s_ref,
    sg_ref,
    sh_hbm,
    order_ref,
    label_ref,
    loss_ref,
    ig_ref,
    a_out,
    g2_ref,
    gath,
    th,
    sh,
    acc,
    rows_a,
    s_snd,
    s_rcv,
    st_own,
    st_rcv,
    scale_ref,
    tl_snd,
    tl_rcv,
    sl_snd,
    sl_rcv,
    g_snd,
    g_rcv,
    sib_snd,
    sib_rcv,
    hb,
    p1_snd,
    p1_rcv,
    h1,
    p2_snd,
    p2_rcv,
    p3_snd,
    p3_rcv,
    ls_own,
    ls_rcv,
    ssem,
    rsem,
    lsem,
    bulk_s,
    bulk_r,
):
    role = lax.axis_index("role")
    vocab = lax.axis_index("vocab")
    me_c = rem(vocab, 2)
    me = (div(vocab, 16), role * 2 + rem(div(vocab, 8), 2), rem(div(vocab, 2), 4))
    flat = role * 64 + vocab
    j_me = me[X] * 2 + me_c
    g_me = me[Y] * 4 + me[Z]

    def device(x, y, z, c):
        return (div(y, 2), ((x * 2 + rem(y, 2)) * 4 + z) * 2 + c)

    def moved(axis, step):
        return rem(me[axis] + step, 4)

    def line(axis, step):
        at = list(me)
        at[axis] = moved(axis, step)
        return device(at[0], at[1], at[2], me_c)

    sibling = device(me[X], me[Y], me[Z], 1 - me_c)

    def column(k):
        return device(div(k, 2), me[Y], me[Z], rem(k, 2))

    def plane(dy, dz):
        return device(me[X], moved(Y, dy), moved(Z, dz), me_c)

    started = []

    def send(src, dst, to):
        k = len(started)
        copy = pltpu.make_async_remote_copy(
            src, dst, ssem.at[k], rsem.at[k], device_id=to, device_id_type=MESH
        )
        copy.start()
        started.append(copy)
        return copy

    plane_steps = [(dy, dz) for dy in range(4) for dz in range(4) if (dy, dz) != (0, 0)]
    barrier = pltpu.get_barrier_semaphore()
    for k in range(1, 8):
        pl.semaphore_signal(barrier, inc=1, device_id=column(rem(j_me + k, 8)), device_id_type=MESH)
    for dy, dz in plane_steps:
        pl.semaphore_signal(barrier, inc=1, device_id=plane(dy, dz), device_id_type=MESH)

    load_sh = pltpu.make_async_copy(sh_hbm, sh, lsem.at[0])
    load_th = pltpu.make_async_copy(th_hbm, th, lsem.at[1])
    load_sh.start()
    load_th.start()

    own = t_ref[...]
    gath[me[X], me[Y], me[Z], me_c] = own
    own_f = own.astype(F32)
    sums = jnp.sum(own_f * own_f, axis=1, keepdims=True)
    flipped = jnp.broadcast_to(sums, (128, 128)).T[:8]
    st_own[0, 0] = jnp.where(role == 0, flipped, 0.0)
    st_own[0, 1] = jnp.where(role == 1, flipped, 0.0)

    stud = s_ref[...].astype(F32)
    stud_scale = lax.rsqrt(jnp.mean(stud * stud, axis=1, keepdims=True) + EPS)
    stud_normed = (stud * stud_scale * sg_ref[...]).astype(BF16)
    for j in range(8):
        s_snd[j] = stud_normed[:, j * 512 : (j + 1) * 512]
    s_rcv[j_me] = s_snd[j_me]

    pl.semaphore_wait(barrier, 22)

    def at(part, a, b, c):
        (first, second, last), start, count = PARTS[part]
        index = [None, None, None]
        index[first], index[second], index[last] = a, b, c
        return gath.at[index[0], index[1], index[2], me_c, pl.ds(start, count)]

    def axes(part):
        return PARTS[part][0]

    parts = range(3)
    steps = (1, 3, 2)

    first = {}
    for p in parts:
        a, b, c = axes(p)
        mine = at(p, me[a], me[b], me[c])
        for d in steps:
            first[p, d] = send(mine, mine, line(a, d))
    spread = []
    for k in range(1, 8):
        to = rem(j_me + k, 8)
        spread.append(send(s_snd.at[to], s_rcv.at[j_me], column(to)))
    stats = [send(st_own.at[0], st_rcv.at[i], line(X, d)) for i, d in enumerate(steps)]

    heavy = {}
    second = {}
    side = []

    def to_side(ref):
        side.append(send(ref, ref, sibling))

    def start_heavy(p, g):
        a, b, c = axes(p)
        group = at(p, ALL, moved(b, (4 - (0, 1, 3, 2)[g]) % 4), me[c])
        heavy[p, g, 1] = send(group, group, line(c, 1))
        heavy[p, g, 3] = send(group, group, line(c, 3))
        to_side(group)

    for p in parts:
        a, b, c = axes(p)
        for d in steps:
            first[p, d].wait_recv()
        group = at(p, ALL, me[b], me[c])
        for d in steps:
            second[p, d] = send(group, group, line(b, d))
        start_heavy(p, 0)

    for copy in spread:
        copy.wait_recv()
    tile = jnp.concatenate([s_rcv[k].astype(F32) for k in range(8)], axis=0)
    rows_a[j_me, g_me] = tile.astype(BF16)
    tile_ref = rows_a.at[j_me, g_me]
    gather_plane = [send(tile_ref, tile_ref, plane(dy, dz)) for dy, dz in plane_steps]

    def add_stats(stage, copies, base):
        total = st_own[stage]
        for i, copy in enumerate(copies):
            copy.wait_recv()
            total = total + st_rcv[base + i]
        st_own[stage + 1] = total

    add_stats(0, stats, 0)
    stats = [send(st_own.at[1], st_rcv.at[3 + i], line(Y, d)) for i, d in enumerate(steps)]

    for g, d in enumerate(steps):
        for p in parts:
            second[p, d].wait_recv()
            start_heavy(p, g + 1)

    add_stats(1, stats, 3)
    stats = [send(st_own.at[2], st_rcv.at[6 + i], line(Z, d)) for i, d in enumerate(steps)]

    for copy in gather_plane:
        copy.wait_recv()
    chunk_ref = rows_a.at[j_me]
    lines_x = {d: send(chunk_ref, chunk_ref, line(X, d)) for d in steps}
    stud_side = [send(chunk_ref, chunk_ref, sibling)]

    halves = {}
    for g in range(4):
        for p in parts:
            a, b, c = axes(p)
            at_b = moved(b, (4 - (0, 1, 3, 2)[g]) % 4)
            for d, half in ((1, pl.ds(0, 2)), (3, pl.ds(2, 2))):
                heavy[p, g, d].wait_recv()
                from_c = moved(c, 4 - d)
                piece = at(p, half, at_b, from_c)
                halves[p, g, d] = send(piece, piece, line(c, d))
                to_side(at(p, ALL, at_b, from_c))
        if g == 0:
            add_stats(2, stats, 6)
            stats = [send(st_own.at[3], st_rcv.at[9], sibling)]

    for d in steps:
        lines_x[d].wait_recv()
        arrived = rows_a.at[moved(X, 4 - d) * 2 + me_c]
        stud_side.append(send(arrived, arrived, sibling))

    for g in range(4):
        for p in parts:
            a, b, c = axes(p)
            at_b = moved(b, (4 - (0, 1, 3, 2)[g]) % 4)
            for d, half in ((1, pl.ds(0, 2)), (3, pl.ds(2, 2))):
                halves[p, g, d].wait_recv()
                to_side(at(p, half, at_b, moved(c, 2)))

    sub = lax.broadcasted_iota(jnp.int32, (8, 128), 0)
    lane = lax.broadcasted_iota(jnp.int32, (8, 128), 1)
    pair = sub // 2

    def to_owner(out, into, r, index, sem):
        rows = acc[pl.ds(pl.multiple_of(r * 8, 8), 8), :]
        tiles = shuffle4([rows[:, j * 128 : (j + 1) * 128] for j in range(4)], pair)
        for k in range(4):
            to = index(r, k)
            out[to] = tiles[k].astype(BF16)

            @pl.when(to != flat)
            def _():
                pltpu.make_async_remote_copy(
                    out.at[to],
                    into.at[flat],
                    bulk_s.at[sem],
                    bulk_r.at[sem],
                    device_id=(div(to, 64), rem(to, 64)),
                    device_id_type=MESH,
                ).start()

            @pl.when(to == flat)
            def _():
                into[to] = out[to]

    def column_index(r, k):
        g = div(r, 2)
        return flat_of(rem(r, 2) * 2 + k // 2, div(g, 4), rem(g, 4), k % 2)

    def plain_index(r, k):
        return r * 4 + k

    def bulk_wait(buf, sems, sem):
        pltpu.make_async_copy(buf.at[pl.ds(0, 127)], buf.at[pl.ds(0, 127)], sems.at[sem]).wait()

    for copy in stud_side:
        copy.wait_recv()
    load_sh.wait()
    for j in range(8):
        part = lax.dot_general(
            rows_a[j].reshape(256, 512),
            sh[:, j * 512 : (j + 1) * 512],
            (((1,), (1,)), ((), ())),
            preferred_element_type=F32,
        )
        if j == 0:
            acc[...] = part
        else:
            acc[...] += part

    @pl.loop(0, 32)
    def _(i):
        to_owner(sl_snd, sl_rcv, rem(i + g_me * 2, 32), column_index, 0)

    add_stats(3, stats, 9)
    for r in range(2):
        scale = lax.rsqrt(st_own[4, r] * (1.0 / 16384) + EPS)
        scale_ref[r] = jnp.broadcast_to(scale[0:1], (128, 128)).T
    load_th.wait()
    for copy in side:
        copy.wait_recv()
    acc[...] = jnp.zeros_like(acc)

    @pl.loop(0, 16)
    def _(kk):
        x = div(kk, 4)
        y_lo = rem(div(kk, 2), 2)
        z2 = rem(kk, 2) * 2
        lanes = []
        for u in range(4):
            gain = tg_ref[pl.ds(kk, 1), u * 256 : (u + 1) * 256]
            halves_ = []
            for r in range(2):
                block = gath[x, 2 * r + y_lo, z2 + u // 2, u % 2].astype(F32)
                scale = scale_ref[r]
                scale = jnp.concatenate([scale, scale], axis=1)
                halves_.append((block * scale * gain).astype(BF16))
            lanes.append(jnp.concatenate(halves_, axis=0))
        left = jnp.concatenate(lanes, axis=1)
        right = th[:, pl.ds(pl.multiple_of(kk * 1024, 1024), 1024)]
        acc[...] += lax.dot_general(
            left, right, (((1,), (1,)), ((), ())), preferred_element_type=F32
        )

    @pl.loop(0, 32)
    def _(i):
        to_owner(tl_snd, tl_rcv, rem(i + div(flat, 4), 32), plain_index, 1)

    outs = []
    for j in range(8):
        out = pltpu.make_async_copy(
            rows_a.at[j], a_out.at[:, :, pl.ds(j * 512, 512)], lsem.at[2 + j]
        )
        out.start()
        outs.append(out)

    def over(value, op, reduce):
        value = jnp.broadcast_to(reduce(value, axis=1, keepdims=True), (8, 128))
        value = op(value, pltpu.roll(value, 2, 0))
        return op(value, pltpu.roll(value, 4, 0))

    def log_sum(ref):
        def top_step(i, top):
            return jnp.maximum(top, jnp.max(ref[pl.ds(i * 16, 16)].astype(F32), axis=0))

        top = lax.fori_loop(0, 8, top_step, jnp.full((8, 128), -jnp.inf, F32))
        top = over(top, jnp.maximum, jnp.max)

        def sum_step(i, total):
            return total + jnp.sum(jnp.exp(ref[pl.ds(i * 16, 16)].astype(F32) - top[None]), axis=0)

        total = lax.fori_loop(0, 8, sum_step, jnp.zeros((8, 128), F32))
        return top + jnp.log(over(total, jnp.add, jnp.sum))

    bulk_wait(sl_rcv, bulk_r, 0)
    stud_log = log_sum(sl_rcv)
    bulk_wait(tl_rcv, bulk_r, 1)
    teach_log = log_sum(tl_rcv)
    token = sub % 2
    wanted = jnp.where(token == 0, label_ref[flat * 2], label_ref[flat * 2 + 1])
    place = pair * 128 + lane

    def term(n, carry):
        i = rem(n + flat, 128)
        teach = tl_rcv[order_ref[i]].astype(F32)
        student = sl_rcv[i].astype(F32)
        teach_prob = jnp.exp(teach - teach_log)
        stud_prob = jnp.exp(student - stud_log)
        hit = (place + i * 512) == wanted
        grad = LOSS_SCALE * (
            (1.0 + CE_WEIGHT) * stud_prob - teach_prob - CE_WEIGHT * hit.astype(F32)
        )
        g_snd[i] = grad.astype(BF16)

        @pl.when(i != flat)
        def _():
            pltpu.make_async_remote_copy(
                g_snd.at[i],
                g_rcv.at[flat],
                bulk_s.at[2],
                bulk_r.at[2],
                device_id=(div(i, 64), rem(i, 64)),
                device_id_type=MESH,
            ).start()

        return carry + teach_prob * (teach - student) - CE_WEIGHT * jnp.where(hit, student, 0.0)

    total = lax.fori_loop(0, 128, term, jnp.zeros((8, 128), F32), unroll=4)
    g_rcv[flat] = g_snd[flat]
    once = (sub < 2) & (lane == 0)
    total = total + jnp.where(once, (1.0 + CE_WEIGHT) * stud_log - teach_log, 0.0)
    total = jnp.sum(jnp.sum(total, axis=1, keepdims=True), axis=0, keepdims=True)
    ls_own[0] = jnp.broadcast_to(total, (8, 128))
    loss_side = send(ls_own.at[0], ls_rcv.at[0], sibling)

    bulk_wait(g_rcv, bulk_r, 2)

    @pl.loop(0, 16)
    def _(g):
        rows = []
        for h in range(2):
            msgs = [g_rcv[column_index(g * 2 + h, k)].astype(F32) for k in range(4)]
            rows.append(jnp.concatenate(shuffle4(msgs, pair), axis=1))
        start = pl.multiple_of(g * 16, 16)
        g2_ref[pl.ds(start, 16), :] = jnp.concatenate(rows, axis=0).astype(BF16)

    def hidden_cols(core, part):
        cols = pl.ds(pl.multiple_of(core * 2048 + part * 1024, 1024), 1024)
        value = jnp.dot(g2_ref[...], sh[:, cols], preferred_element_type=F32)
        return value.reshape(4, 4, 16, 1024)

    sides = []
    for part in range(2):
        sib_snd[part] = hidden_cols(1 - me_c, part).astype(BF16)
        sides.append(send(sib_snd.at[part], sib_rcv.at[part], sibling))
    for part in range(2):
        hb[part] = hidden_cols(me_c, part)

    def add_loss(stage, copies, base, axis):
        for copy in copies:
            copy.wait_recv()
        total = jnp.zeros((8, 128), F32)
        for i in range(4):
            total = total + jnp.where(me[axis] == i, ls_own[stage], ls_rcv[base + i])
        ls_own[stage + 1] = total

    def spread_loss(stage, base, axis):
        return [
            send(ls_own.at[stage], ls_rcv.at[base + me[axis]], line(axis, d)) for d in steps
        ]

    loss_side.wait_recv()
    ls_own[1] = ls_own[0] + ls_rcv[0]
    for i in range(3):
        ls_rcv[1 + 4 * i + me[(Y, Z, X)[i]]] = jnp.zeros((8, 128), F32)

    phase1 = {}
    for part, axis in enumerate((Y, Z)):
        sides[part].wait_recv()
        summed = hb[part] + sib_rcv[part].astype(F32)
        hb[part] = summed
        p1_snd[part] = (summed if axis == Y else jnp.swapaxes(summed, 0, 1)).astype(BF16)
        for i, d in enumerate(steps):
            phase1[part, i] = send(p1_snd.at[part, moved(axis, d)], p1_rcv.at[part, i], line(axis, d))
    loss_copies = spread_loss(1, 1, Y)

    phase2 = {}
    for part, axis in enumerate((Y, Z)):
        other = (Z, Y)[part]
        total = hb[0, me[Y]] if axis == Y else hb[1, :, me[Z]]
        for i in range(3):
            phase1[part, i].wait_recv()
            total = total + p1_rcv[part, i].astype(F32)
        h1[part] = total
        p2_snd[part] = total.astype(BF16)
        for i, d in enumerate(steps):
            phase2[part, i] = send(p2_snd.at[part, moved(other, d)], p2_rcv.at[part, i], line(other, d))
    add_loss(1, loss_copies, 1, Y)
    loss_copies = spread_loss(2, 5, Z)

    for part in range(2):
        other = (Z, Y)[part]
        total = h1[part, me[other]]
        for i in range(3):
            phase2[part, i].wait_recv()
            total = total + p2_rcv[part, i].astype(F32)
        for k in range(8):
            p3_snd[k, :, part * 1024 : (part + 1) * 1024] = total[2 * k : 2 * k + 2]
    phase3 = []
    for k in range(1, 8):
        to = rem(j_me + k, 8)
        phase3.append(send(p3_snd.at[to], p3_rcv.at[j_me], column(to)))
    p3_rcv[j_me] = p3_snd[j_me]
    add_loss(2, loss_copies, 5, Z)
    loss_copies = spread_loss(3, 9, X)
    for copy in phase3:
        copy.wait_recv()
    back = [
        p3_rcv[c] + p3_rcv[2 + c] + p3_rcv[4 + c] + p3_rcv[6 + c] for c in range(2)
    ]
    back = jnp.concatenate(back, axis=1) * sg_ref[...]
    hat = s_ref[...].astype(F32) * stud_scale
    ig_ref[...] = stud_scale * (back - hat * jnp.mean(back * hat, axis=1, keepdims=True))
    add_loss(3, loss_copies, 9, X)
    loss_ref[...] = ls_own[4] * (1.0 / 256)

    for copy in started:
        copy.wait_send()
    for k, buf in enumerate((sl_snd, tl_snd, g_snd)):
        bulk_wait(buf, bulk_s, k)
    for out in outs:
        out.wait()


def positions(mapping, wanted):
    count = mapping.shape[0]
    match = mapping[None, :] == wanted[:, None]
    return jnp.sum(jnp.where(match, jnp.arange(count, dtype=jnp.int32)[None, :], 0), axis=1)


def body(
    teacher_hidden,
    teacher_gain,
    teacher_head,
    student_hidden,
    student_gain,
    student_head,
    token_ids,
    teacher_map,
    student_map,
):
    order = positions(teacher_map, student_map)
    label_col = positions(student_map, token_ids // 512) * 512 + token_ids % 512
    vmem = pl.BlockSpec(memory_space=pltpu.VMEM)
    smem = pl.BlockSpec(memory_space=pltpu.SMEM)
    hbm = pl.BlockSpec(memory_space=pl.ANY)
    loss, input_grad, rows, grad = pl.pallas_call(
        kernel,
        out_shape=(
            jax.ShapeDtypeStruct((8, 128), F32),
            jax.ShapeDtypeStruct((2, 4096), F32),
            jax.ShapeDtypeStruct((16, 16, 4096), BF16),
            jax.ShapeDtypeStruct((256, 512), BF16),
        ),
        in_specs=[vmem, vmem, hbm, vmem, vmem, hbm, smem, smem],
        out_specs=(vmem, vmem, hbm, vmem),
        scratch_shapes=[
            pltpu.VMEM((4, 4, 4, 2, 128, 256), BF16),
            pltpu.VMEM((512, 16384), BF16),
            pltpu.VMEM((512, 4096), BF16),
            pltpu.VMEM((256, 512), F32),
            pltpu.VMEM((8, 16, 16, 512), BF16),
            pltpu.VMEM((8, 2, 512), BF16),
            pltpu.VMEM((8, 2, 512), BF16),
            pltpu.VMEM((5, 2, 8, 128), F32),
            pltpu.VMEM((10, 2, 8, 128), F32),
            pltpu.VMEM((2, 128, 128), F32),
            pltpu.VMEM((128, 8, 128), BF16),
            pltpu.VMEM((128, 8, 128), BF16),
            pltpu.VMEM((128, 8, 128), BF16),
            pltpu.VMEM((128, 8, 128), BF16),
            pltpu.VMEM((128, 8, 128), BF16),
            pltpu.VMEM((128, 8, 128), BF16),
            pltpu.VMEM((2, 4, 4, 16, 1024), BF16),
            pltpu.VMEM((2, 4, 4, 16, 1024), BF16),
            pltpu.VMEM((2, 4, 4, 16, 1024), F32),
            pltpu.VMEM((2, 4, 4, 16, 1024), BF16),
            pltpu.VMEM((2, 3, 4, 16, 1024), BF16),
            pltpu.VMEM((2, 4, 16, 1024), F32),
            pltpu.VMEM((2, 4, 16, 1024), BF16),
            pltpu.VMEM((2, 3, 16, 1024), BF16),
            pltpu.VMEM((8, 2, 2048), F32),
            pltpu.VMEM((8, 2, 2048), F32),
            pltpu.VMEM((5, 8, 128), F32),
            pltpu.VMEM((13, 8, 128), F32),
            pltpu.SemaphoreType.DMA((N_SEM,)),
            pltpu.SemaphoreType.DMA((N_SEM,)),
            pltpu.SemaphoreType.DMA((10,)),
            pltpu.SemaphoreType.DMA((3,)),
            pltpu.SemaphoreType.DMA((3,)),
        ],
        compiler_params=pltpu.CompilerParams(
            collective_id=0, has_side_effects=True, vmem_limit_bytes=60 << 20
        ),
        cost_estimate=pl.CostEstimate(
            flops=2 * 256 * 512 * (16384 + 2 * 4096), bytes_accessed=24 << 20, transcendentals=0
        ),
        name="distill",
    )(
        teacher_hidden,
        teacher_gain.astype(F32).reshape(16, 1024),
        teacher_head,
        student_hidden,
        student_gain.astype(F32).reshape(1, 4096),
        student_head,
        order,
        label_col,
    )
    head_grad = lax.dot_general(
        grad, rows.reshape(256, 4096), (((0,), (0,)), ((), ())), preferred_element_type=F32
    ).astype(BF16)
    return (loss[0, 0], head_grad, input_grad)


def solution(mesh):
    placed = (
        P("role", "vocab"),
        P(),
        P(("role", "vocab"), None),
        P(("role", "vocab"), None),
        P(),
        P(("role", "vocab"), None),
        P(),
        P(),
        P(),
    )
    return jax.shard_map(
        body,
        mesh=mesh,
        in_specs=placed,
        out_specs=(P(), P(("role", "vocab"), None), P(("role", "vocab"), None)),
        check_vma=False,
    )
```

time: 559 us -> 109 us (0.19)
  waiting for transfers between devices: 390 us -> 0 us
  Pallas kernels: 0 us -> 94.4 us
  blocking collectives: 85.6 us -> 0 us
  matrix products: 26.3 us -> 4.98 us
  between operations: 15.6 us -> 0.65 us
  starting transfers between devices: 13.8 us -> 0 us
  other arithmetic: 18.2 us -> 5.44 us
    all_gather x2 -> x0, waiting for transfers between devices: 298 us -> none  [the longest x1 187 us: body(): lax.all_gather(student_hidden, ('role', 'vocab'), axis=0, tiled=True)]
    pallas_call x0 -> x1, Pallas kernels: none -> 94.4 us  [body(): pl.pallas_call(kernel, out_shape=(jax.ShapeDtypeStruct((8, 128), F32), ja...]
    unnamed x4 -> x0, waiting for transfers between devices: 81.9 us -> none
    psum x1 -> x0, blocking collectives: 62.6 us -> none  [body(): loss = lax.psum(jnp.sum(per_token), ('role', 'vocab')) / tokens_all]
    dot_general x4 -> x1, matrix products: 26.3 us -> 4.98 us  [body(): lax.dot_general(grad, rows.reshape(256, 4096), (((0,), (0,)), ((), ())),...]
    all_to_all x1 -> x0, blocking collectives: 15.1 us -> none  [body(): lax.all_to_all(grad_tokens, ('role', 'vocab'), split_axis=1, concat_axis=...]
    all_to_all x2 -> x0, starting transfers between devices: 13.7 us -> none  [the longest x1 7.01 us: body(): lax.all_to_all(student_logits, ('role', 'vocab'), split_axis=0, concat_ax...]
    all_to_all x2 -> x0, waiting for transfers between devices: 10.6 us -> none  [the longest x1 10.6 us: body(): lax.all_to_all(teacher_logits, ('role', 'vocab'), split_axis=0, concat_ax...]
  transfers between devices with their start and end apart: 5 -> 0, of which waited for: 4 -> 0; matrix products, arithmetic and copies ran while one was open for 7% -> 0% of each run, Pallas kernels for 0% -> 0%
where the time goes in v1:
time: 109 us
  Pallas kernels  94.4 us (87%)
  other arithmetic  5.44 us (5%)
  matrix products  4.98 us (5%)
  local copies, waits for them, and re-layouts  3.22 us (3%)
    pallas_call x1, Pallas kernels, body(): pl.pallas_call(kernel, out_shape=(jax.ShapeDtypeStruct((8, 128), F32), ja...  94.4 us
    dot_general x1, matrix products, body(): lax.dot_general(grad, rows.reshape(256, 4096), (((0,), (0,)), ((), ())),...  4.98 us
    reduce_sum x2, other arithmetic, positions(): jnp.sum(jnp.where(match, jnp.arange(count, dtype=jnp.int32)[None, :], 0),...  2.19 us

profile of v1, /device:TPU:1, one launch (start us, length us, event | category | flops | bytes accessed | tf_op | source)
XLA Modules:
  0.0 108.7 jit_solution(16503455474821389928)
XLA Ops:
  0.6 1.4 %select_reduce_fusion.1.order_ref = s32[128]{0:T(128)} fusion(s32[128]{0:T(128)} %param.16, s32[128]{0:T(128)} %param.17), kind=kLoop, calls=%fused_computation.2 | loop fusion | flops 49024 | bytes 1536 | tf_op jit(solution)/shard_map/reduce_sum | solution.py:522
  2.0 0.7 and_select_fusion.1
  2.7 0.8 select_reduce_fusion
  3.5 1.3 %fusion.label_ref = s32[256]{0:T(256)} fusion(s32[256]{0:T(256)S(1)} %select_reduce_fusion, s32[256]{0:T(256)} %param.15), kind=kLoop, calls=%fused_computation.8 | loop fusion | flops 3328 | bytes 3072 | tf_op jit(solution)/shard_map/add | solution.py:537
  4.8 1.3 %reshape.30 = f32[4096]{0:T(1024)} convert(bf16[4096]{0:T(1024)(128)(2,1)} %param.13) | non-fusion elementwise | flops 4096 | bytes 24576 | tf_op jit(solution)/shard_map/reshape | solution.py:598
  6.1 1.4 %reshape.29.tg_ref = f32[16,1024]{1,0:T(8,128)} reshape(bf16[16384]{0:T(1024)(128)(2,1)} %param.10) | data formatting | bytes 98304 | tf_op jit(solution)/shard_map/reshape | solution.py:595
  7.5 94.4 %distill.1 = (f32[8,128]{1,0:T(8,128)}, f32[2,4096]{1,0:T(2,128)}, bf16[16,16,4096]{2,1,0:T(8,128)(2,1)}, bf16[256,512]{1,0:T(8,128)(2,1)}) custom-call(bf16[128,256]{1,0:T(8,128)(2,1)} %t_ref.1, f32[16,1024]{1,0:T(8,128)} %reshape.29.tg_ref, bf16[512,16384]{1,0:T(8,128)(2,1)} %th_hbm.1, bf16[2,4096]{1,0:T(2,128)(2,1)} %s_ref.1, f32[1,4096]{1,0:T(1,128)} %bitcast.6, ...), custom_call_target="tpu_custom_call" | custom-call | flops 6442450944 | bytes 25165824 | tf_op jit(solution)/shard_map/distill/pallas_call | solution.py:541
  101.9 0.0 copy-start
  101.9 1.2 %slice.3 = f32[1,1]{1,0:T(1,128)} slice(f32[8,128]{1,0:T(8,128)} %get-tuple-element.7), slice={[0:1], [0:1]} | slice | bytes 8 | tf_op jit(solution)/shard_map/slice | solution.py:606
  103.1 5.0 %convolution_convert_fusion = bf16[512,4096]{1,0:T(8,128)(2,1)} fusion(bf16[256,512]{1,0:T(8,128)(2,1)} %get-tuple-element.8, bf16[256,4096]{1,0:T(8,128)(2,1)} %bitcast.5), kind=kOutput, calls=%fused_computation | convolution fusion | flops 1075838976 | bytes 6553600 | tf_op jit(solution)/shard_map/dot_general | solution.py:603
  108.1 0.0 copy-done
  108.1 0.6 copy.13
Async XLA Ops:
  101.9 6.2 %copy-start = (f32[2,4096]{1,0:T(2,128)S(1)}, f32[2,4096]{1,0:T(2,128)}, u32[]{:S(2)}) copy-start(f32[2,4096]{1,0:T(2,128)} %get-tuple-element.16) | copy-start | bytes 98308

commit v2 on v1

v2 whole, which is shorter than its diff:
```python
import jax
import jax.numpy as jnp
from jax import lax
from jax.experimental import pallas as pl
from jax.experimental.pallas import tpu as pltpu
from jax.sharding import PartitionSpec as P

EPS = 1e-05
LOSS_SCALE = 256.0
CE_WEIGHT = 0.25
MESH = pl.DeviceIdType.MESH
F32 = jnp.float32
BF16 = jnp.bfloat16
X, Y, Z = 0, 1, 2
ALL = pl.ds(0, 4)
PARTS = (((Y, Z, X), 0, 32), ((X, Z, Y), 32, 48), ((Y, X, Z), 80, 48))
SEND = {name: k for k, name in enumerate(
    ("spread", "plane", "ring", "stud_side", "first", "second", "last", "side", "stats", "loss", "sib", "line", "direct")
)}
RECV_COUNTS = dict(
    spread=1, plane=1, ring=4, far=1, stud_side=1, first=9, second=9, heavy=24, halves=12,
    side=2, stats=4, loss=4, sib=4, line=4, direct=2,
)
RECV = {name: sum(list(RECV_COUNTS.values())[:k]) for k, name in enumerate(RECV_COUNTS)}
N_RECV = sum(RECV_COUNTS.values())


def div(a, b):
    return lax.div(a, jnp.int32(b))


def rem(a, b):
    return lax.rem(a, jnp.int32(b))


def flat_of(x, y, z, c):
    return div(y, 2) * 64 + ((x * 2 + rem(y, 2)) * 4 + z) * 2 + c


def shuffle4(tiles, pair):
    out = []
    for b in range(4):
        acc = None
        for a in range(4):
            shift = (2 * (a - b)) % 8
            moved = pltpu.roll(tiles[a], shift, 0) if shift else tiles[a]
            acc = moved if acc is None else jnp.where(pair == a, moved, acc)
        out.append(acc)
    return out


def kernel(
    t_hbm,
    tg_hbm,
    th_hbm,
    s_hbm,
    sg_hbm,
    sh_hbm,
    ids_hbm,
    tm_hbm,
    sm_hbm,
    loss_ref,
    ig_ref,
    g2t_out,
    rows_out,
    gath,
    th,
    sh,
    tg,
    sg,
    s_ref,
    tmap,
    smap,
    order_vec,
    ids,
    order_ref,
    acc,
    acc_s,
    rows_a,
    s_snd,
    s_rcv,
    st_own,
    st_rcv,
    scale_ref,
    tl_snd,
    tl_rcv,
    sl_snd,
    sl_rcv,
    g_snd,
    g_rcv,
    g2_ref,
    g2t,
    sib_snd,
    sib_rcv,
    hb,
    p1_snd,
    p1_rcv,
    p2_snd,
    p2_rcv,
    ls_own,
    ls_rcv,
    ssem,
    rsem,
    lsem,
    bulk_s,
    bulk_r,
):
    role = lax.axis_index("role")
    vocab = lax.axis_index("vocab")
    me_c = rem(vocab, 2)
    me = (div(vocab, 16), role * 2 + rem(div(vocab, 8), 2), rem(div(vocab, 2), 4))
    flat = role * 64 + vocab
    j_me = me[X] * 2 + me_c
    g_me = me[Y] * 4 + me[Z]

    def device(x, y, z, c):
        return (div(y, 2), ((x * 2 + rem(y, 2)) * 4 + z) * 2 + c)

    def moved(axis, step):
        return rem(me[axis] + step, 4)

    def line(axis, step):
        at = list(me)
        at[axis] = moved(axis, step)
        return device(at[0], at[1], at[2], me_c)

    sibling = device(me[X], me[Y], me[Z], 1 - me_c)

    def column(k):
        return device(div(k, 2), me[Y], me[Z], rem(k, 2))

    def plane(dy, dz):
        return device(me[X], moved(Y, dy), moved(Z, dz), me_c)

    def send(src, dst, to, group, index=0, sender=None):
        pltpu.make_async_remote_copy(
            src,
            dst,
            ssem.at[SEND[sender or group]],
            rsem.at[RECV[group] + index],
            device_id=to,
            device_id_type=MESH,
        ).start()

    def arrived(ref, group, index=0):
        pltpu.make_async_copy(ref, ref, rsem.at[RECV[group] + index]).wait()

    def left(ref, sender):
        pltpu.make_async_copy(ref, ref, ssem.at[SEND[sender]]).wait()

    plane_steps = [(dy, dz) for dy in range(4) for dz in range(4) if (dy, dz) != (0, 0)]
    barrier = pltpu.get_barrier_semaphore()
    for k in range(1, 8):
        pl.semaphore_signal(barrier, inc=1, device_id=column(rem(j_me + k, 8)), device_id_type=MESH)
    for dy, dz in plane_steps:
        pl.semaphore_signal(barrier, inc=1, device_id=plane(dy, dz), device_id_type=MESH)

    own_slot = gath.at[me[X], me[Y], me[Z], me_c]
    loads = [
        pltpu.make_async_copy(src, dst, lsem.at[k])
        for k, (src, dst) in enumerate(
            (
                (t_hbm, own_slot),
                (s_hbm, s_ref),
                (sg_hbm, sg),
                (tg_hbm, tg),
                (tm_hbm, tmap),
                (sm_hbm, smap),
                (ids_hbm, ids),
                (sh_hbm, sh),
                (th_hbm, th),
            )
        )
    ]
    for load in loads[:7]:
        load.start()
    load_sh, load_th = loads[7:]

    loads[1].wait()
    loads[2].wait()
    stud = s_ref[...].astype(F32)
    stud_gain = sg[...].astype(F32).reshape(1, 4096)
    stud_scale = lax.rsqrt(jnp.mean(stud * stud, axis=1, keepdims=True) + EPS)
    stud_normed = (stud * stud_scale * stud_gain).astype(BF16)
    for j in range(8):
        s_snd[j] = stud_normed[:, j * 512 : (j + 1) * 512]
    s_rcv[j_me] = s_snd[j_me]
    loads[0].wait()

    pl.semaphore_wait(barrier, 22)

    def at(part, a, b, c):
        (first, second, last), start, count = PARTS[part]
        index = [None, None, None]
        index[first], index[second], index[last] = a, b, c
        return gath.at[index[0], index[1], index[2], me_c, pl.ds(start, count)]

    def axes(part):
        return PARTS[part][0]

    parts = range(3)
    steps = (1, 3, 2)

    for k in range(1, 8):
        to = rem(j_me + k, 8)
        send(s_snd.at[to], s_rcv.at[j_me], column(to), "spread")

    def no(p, d):
        return p * 3 + steps.index(d)

    def last_no(p, g, d):
        return (p * 4 + g) * 2 + d // 2

    def mine(p):
        a, b, c = axes(p)
        return at(p, me[a], me[b], me[c])

    for p in parts:
        a, b, c = axes(p)
        for d in steps:
            send(mine(p), mine(p), line(a, d), "first", no(p, d))
    for p in parts:
        a, b, c = axes(p)
        for d in (1, 3):
            send(mine(p), mine(p), line(c, d), "heavy", last_no(p, 0, d), "last")
        for d in steps:
            send(mine(p), mine(p), line(b, d), "second", no(p, d))
    own_f = own_slot[...].astype(F32)
    sums = jnp.sum(own_f * own_f, axis=1, keepdims=True)
    flipped = jnp.broadcast_to(sums, (128, 128)).T[:8]
    st_own[0, 0] = jnp.where(role == 0, flipped, 0.0)
    st_own[0, 1] = jnp.where(role == 1, flipped, 0.0)

    def spread_stats(stage):
        for i, d in enumerate(steps):
            send(st_own.at[stage], st_rcv.at[stage * 3 + i], line((X, Y, Z)[stage], d), "stats", stage)

    def add_stats(stage):
        arrived(st_rcv.at[pl.ds(stage * 3, 3)], "stats", stage)
        total = st_own[stage]
        for i in range(3):
            total = total + st_rcv[stage * 3 + i]
        st_own[stage + 1] = total

    spread_stats(0)

    def to_side(g, ref):
        send(ref, ref, sibling, "side", g // 3)

    def to_stud_side(ref):
        send(ref, ref, sibling, "stud_side")

    def offset_b(p, g):
        return moved(axes(p)[1], (0, 3, 1, 2)[g])

    arrived(s_rcv.at[pl.ds(0, 7)], "spread")
    tile = jnp.concatenate([s_rcv[k].astype(F32) for k in range(8)], axis=0)
    rows_a[j_me, g_me] = tile.astype(BF16)
    tile_ref = rows_a.at[j_me, g_me]
    for dy, dz in plane_steps:
        send(tile_ref, tile_ref, plane(dy, dz), "plane")

    for d in steps:
        for p in parts:
            a, b, c = axes(p)
            block = at(p, moved(a, 4 - d), me[b], me[c])
            arrived(block, "first", no(p, d))
            for e in steps:
                send(block, block, line(b, e), "second", no(p, e))
            for e in (1, 3):
                send(block, block, line(c, e), "heavy", last_no(p, 0, e), "last")
    add_stats(0)
    spread_stats(1)
    for p in parts:
        a, b, c = axes(p)
        to_side(0, at(p, ALL, me[b], me[c]))

    low, high = pl.ds(0, 8), pl.ds(8, 8)
    ways = ((1, low, 0), (3, high, 1), (1, high, 2), (3, low, 3))

    def chunk(step, half=pl.ds(0, 16)):
        return rows_a.at[moved(X, step) * 2 + me_c, half]

    arrived(rows_a.at[j_me, pl.ds(0, 15)], "plane")
    for d, half, n in ways:
        send(chunk(0, half), chunk(0, half), line(X, d), "ring", n)
    to_stud_side(chunk(0))

    for g, d in enumerate(steps):
        for p in parts:
            a, b, c = axes(p)
            group = at(p, ALL, offset_b(p, g + 1), me[c])
            arrived(group, "second", no(p, d))
            for e in (1, 3):
                send(group, group, line(c, e), "heavy", last_no(p, g + 1, e), "last")
            to_side(g + 1, group)
    add_stats(1)
    spread_stats(2)

    for load in loads[7:]:
        load.start()

    for load in loads[3:7]:
        load.wait()
    held = jnp.broadcast_to(tmap[...].astype(F32).reshape(1, 128), (128, 128)).T
    student_map = smap[...].astype(F32).reshape(1, 128)
    down = lax.broadcasted_iota(jnp.int32, (128, 128), 0).astype(F32)
    found = jnp.max(jnp.where(held == student_map, down, 0.0), axis=0, keepdims=True)
    order_vec[...] = jnp.broadcast_to(found, (8, 128)).astype(jnp.int32)
    load_order = pltpu.make_async_copy(order_vec, order_ref, lsem.at[9])
    load_order.start()

    two = ((1, pl.ds(0, 2)), (3, pl.ds(2, 2)))

    def pass_heavy(g):
        for p in parts:
            c = axes(p)[2]
            for d, half in two:
                from_c = moved(c, 4 - d)
                group = at(p, ALL, offset_b(p, g), from_c)
                arrived(group, "heavy", last_no(p, g, d))
                piece = at(p, half, offset_b(p, g), from_c)
                send(piece, piece, line(c, d), "halves", p * 4 + g, "last")
                to_side(g, group)

    def pass_halves(g):
        for p in parts:
            c = axes(p)[2]
            group = at(p, ALL, offset_b(p, g), moved(c, 2))
            arrived(group, "halves", p * 4 + g)
            to_side(g, group)

    pass_heavy(0)
    add_stats(2)
    send(st_own.at[3], st_rcv.at[9], sibling, "stats", 3)
    for d, half, n in ways[:2]:
        piece = chunk(4 - d, half)
        arrived(piece, "ring", n)
        send(piece, piece, line(X, d), "far", 0, "ring")
        to_stud_side(piece)
    pass_heavy(1)
    for d, half, n in ways[2:]:
        piece = chunk(4 - d, half)
        arrived(piece, "ring", n)
        to_stud_side(piece)
    pass_halves(0)
    arrived(chunk(2), "far")
    to_stud_side(chunk(2))
    arrived(st_rcv.at[9], "stats", 3)
    for r in range(2):
        total = st_own[3, r] + st_rcv[9, r]
        scale = lax.rsqrt(total * (1.0 / 16384) + EPS)
        scale_ref[r] = jnp.broadcast_to(scale[0:1], (128, 128)).T
    pass_heavy(2)
    pass_halves(1)

    sub = lax.broadcasted_iota(jnp.int32, (8, 128), 0)
    lane = lax.broadcasted_iota(jnp.int32, (8, 128), 1)
    pair = sub // 2

    def start_bulk(src, dst, to, sem):
        pltpu.make_async_remote_copy(
            src,
            dst,
            bulk_s.at[sem],
            bulk_r.at[sem],
            device_id=(div(to, 64), rem(to, 64)),
            device_id_type=MESH,
        ).start()

    def fill_messages(source, out, r, index):
        rows = source[pl.ds(pl.multiple_of(r * 8, 8), 8), :]
        tiles = shuffle4([rows[:, j * 128 : (j + 1) * 128] for j in range(4)], pair)
        for k in range(4):
            out[index(r, jnp.int32(k))] = tiles[k].astype(BF16)

    def to_owners(source, out, into, own_r, own_k, index, sem, i):
        r = rem(own_r + i, 32)
        fill_messages(source, out, r, index)
        for k in range(4):
            to = index(r, jnp.int32(k))
            start_bulk(out.at[to], into.at[flat], to, sem)

    def to_near_owners(source, out, into, own_r, own_k, index, sem):
        fill_messages(source, out, own_r, index)
        into[flat] = out[flat]
        for i in range(1, 4):
            to = index(own_r, rem(own_k + i, 4))
            start_bulk(out.at[to], into.at[flat], to, sem)

    def column_index(r, k):
        g = div(r, 2)
        return flat_of(rem(r, 2) * 2 + div(k, 2), div(g, 4), rem(g, 4), rem(k, 2))

    def plain_index(r, k):
        return r * 4 + k

    def bulk_wait(buf, sems, sem):
        pltpu.make_async_copy(buf.at[pl.ds(0, 127)], buf.at[pl.ds(0, 127)], sems.at[sem]).wait()

    arrived(rows_a.at[pl.ds(0, 4)], "stud_side")
    load_sh.wait()
    for j in range(8):
        part = lax.dot_general(
            rows_a[j].reshape(256, 512),
            sh[:, j * 512 : (j + 1) * 512],
            (((1,), (1,)), ((), ())),
            preferred_element_type=F32,
        )
        if j == 0:
            acc_s[...] = part
        else:
            acc_s[...] += part
    stud_args = (acc_s, sl_snd, sl_rcv, g_me * 2 + div(me[X], 2), rem(me[X], 2) * 2 + me_c, column_index, 0)
    pass_heavy(3)
    pass_halves(2)
    outs = [pltpu.make_async_copy(rows_a, rows_out, lsem.at[10])]
    outs[0].start()

    load_th.wait()
    arrived(gath.at[pl.ds(0, 3), :, :, 0], "side", 0)
    acc[...] = jnp.zeros_like(acc)

    def teacher_step(dx, dz):
        x, z = rem(me[X] + dx, 4), rem(me[Z] + dz, 4)
        total = None
        for y_lo in range(2):
            base = pl.multiple_of(x * 4096 + y_lo * 2048 + z * 512, 512)
            gain = tg[pl.ds(base, 512)].astype(F32).reshape(1, 512)
            lanes = []
            for c in range(2):
                rows = []
                for r in range(2):
                    block = gath[x, 2 * r + y_lo, z, c].astype(F32)
                    scale = scale_ref[r]
                    scale = jnp.concatenate([scale, scale], axis=1)
                    rows.append((block * scale * gain[:, c * 256 : (c + 1) * 256]).astype(BF16))
                lanes.append(jnp.concatenate(rows, axis=0))
            part = lax.dot_general(
                jnp.concatenate(lanes, axis=1),
                th[:, pl.ds(base, 512)],
                (((1,), (1,)), ((), ())),
                preferred_element_type=F32,
            )
            total = part if total is None else total + part
        acc[...] += total

    @pl.loop(0, 9)
    def _(i):
        q, w = div(i, 3), rem(i, 3)
        for n in range(1, 4):
            to_owners(*stud_args, i * 3 + n)
        teacher_step(q + div(q, 2), w + div(w, 2))

    pass_halves(3)

    @pl.loop(28, 32)
    def _(i):
        to_owners(*stud_args, i)

    to_near_owners(*stud_args)
    arrived(gath.at[0, :, :, 0], "side", 1)

    @pl.loop(0, 4)
    def _(i):
        teacher_step(2, i)

    @pl.loop(0, 3)
    def _(q):
        teacher_step(q + div(q, 2), 2)

    teach_args = (acc, tl_snd, tl_rcv, div(flat, 4), rem(flat, 4), plain_index, 1)

    @pl.loop(1, 32)
    def _(i):
        to_owners(*teach_args, i)

    to_near_owners(*teach_args)

    def over(value, op, reduce):
        value = jnp.broadcast_to(reduce(value, axis=1, keepdims=True), (8, 128))
        value = op(value, pltpu.roll(value, 2, 0))
        return op(value, pltpu.roll(value, 4, 0))

    def log_sum(ref):
        def top_step(i, top):
            return jnp.maximum(top, jnp.max(ref[pl.ds(i * 16, 16)].astype(F32), axis=0))

        top = lax.fori_loop(0, 8, top_step, jnp.full((8, 128), -jnp.inf, F32))
        top = over(top, jnp.maximum, jnp.max)

        def sum_step(i, total):
            return total + jnp.sum(jnp.exp(ref[pl.ds(i * 16, 16)].astype(F32) - top[None]), axis=0)

        total = lax.fori_loop(0, 8, sum_step, jnp.zeros((8, 128), F32))
        return top + jnp.log(over(total, jnp.add, jnp.sum))

    load_order.wait()
    bulk_wait(sl_rcv, bulk_r, 0)
    stud_log = log_sum(sl_rcv)
    bulk_wait(tl_rcv, bulk_r, 1)
    teach_log = log_sum(tl_rcv)
    token = sub % 2
    lane_row = lax.broadcasted_iota(jnp.int32, (1, 128), 1).astype(F32)

    def label_place(label):
        block = div(label, 512)
        match = smap[...].astype(F32).reshape(1, 128) == block.astype(F32)
        place = jnp.sum(jnp.where(match, lane_row, 0.0), axis=1, keepdims=True)
        return place.astype(jnp.int32) * 512 + (label - block * 512)

    wanted = jnp.where(token == 0, label_place(ids[flat * 2]), label_place(ids[flat * 2 + 1]))
    place = pair * 128 + lane

    def term(n, carry):
        i = rem(n + flat, 128)
        teach = tl_rcv[jnp.clip(order_ref[0, i], 0, 127)].astype(F32)
        student = sl_rcv[i].astype(F32)
        teach_prob = jnp.exp(teach - teach_log)
        stud_prob = jnp.exp(student - stud_log)
        hit = (place + i * 512) == wanted
        grad = LOSS_SCALE * (
            (1.0 + CE_WEIGHT) * stud_prob - teach_prob - CE_WEIGHT * hit.astype(F32)
        )
        g_snd[i] = grad.astype(BF16)
        return carry + teach_prob * (teach - student) - CE_WEIGHT * jnp.where(hit, student, 0.0)

    def term_and_send(n, carry):
        carry = term(n, carry)
        i = rem(n + flat, 128)
        start_bulk(g_snd.at[i], g_rcv.at[flat], i, 2)
        return carry

    total = lax.fori_loop(1, 127, term_and_send, jnp.zeros((8, 128), F32), unroll=6)
    total = term_and_send(jnp.int32(127), total)
    total = term(jnp.int32(0), total)
    g_rcv[flat] = g_snd[flat]
    once = (sub < 2) & (lane == 0)
    total = total + jnp.where(once, (1.0 + CE_WEIGHT) * stud_log - teach_log, 0.0)
    total = jnp.sum(jnp.sum(total, axis=1, keepdims=True), axis=0, keepdims=True)
    ls_own[0] = jnp.broadcast_to(total, (8, 128))
    send(ls_own.at[0], ls_rcv.at[0], sibling, "loss", 0)

    def add_loss(stage):
        base = 4 * stage - 3
        axis = (Y, Z, X)[stage - 1]
        arrived(ls_rcv.at[pl.ds(base, 3)], "loss", stage)
        total = jnp.zeros((8, 128), F32)
        for i in range(4):
            total = total + jnp.where(me[axis] == i, ls_own[stage], ls_rcv[base + i])
        ls_own[stage + 1] = total

    def spread_loss(stage):
        base = 4 * stage - 3
        axis = (Y, Z, X)[stage - 1]
        for d in steps:
            send(ls_own.at[stage], ls_rcv.at[base + me[axis]], line(axis, d), "loss", stage)

    for i in range(3):
        ls_rcv[1 + 4 * i + me[(Y, Z, X)[i]]] = jnp.zeros((8, 128), F32)
    arrived(ls_rcv.at[0], "loss", 0)
    ls_own[1] = ls_own[0] + ls_rcv[0]
    spread_loss(1)

    bulk_wait(g_rcv, bulk_r, 2)

    @pl.loop(0, 16)
    def _(g):
        rows = []
        for h in range(2):
            msgs = [g_rcv[column_index(g * 2 + h, k)].astype(F32) for k in range(4)]
            rows.append(jnp.concatenate(shuffle4(msgs, pair), axis=1))
        start = pl.multiple_of(g * 16, 16)
        g2_ref[pl.ds(start, 16), :] = jnp.concatenate(rows, axis=0).astype(BF16)

    def hidden_cols(core, part):
        cols = pl.ds(pl.multiple_of(core * 2048 + part * 512, 512), 512)
        value = jnp.dot(g2_ref[...], sh[:, cols], preferred_element_type=F32)
        return value.reshape(4, 4, 16, 512)

    for part in range(4):
        sib_snd[part] = hidden_cols(1 - me_c, part).astype(BF16)
        send(sib_snd.at[part], sib_rcv.at[part], sibling, "sib", part)
    for part in range(4):
        hb[part] = hidden_cols(me_c, part)
    add_loss(1)
    spread_loss(2)

    for part in range(4):
        axis = (Y, Z)[part % 2]
        arrived(sib_rcv.at[part], "sib", part)
        summed = hb[part] + sib_rcv[part].astype(F32)
        hb[part] = summed
        p1_snd[part] = (summed if axis == Y else jnp.swapaxes(summed, 0, 1)).astype(BF16)
        for i, d in enumerate(steps):
            send(p1_snd.at[part, moved(axis, d)], p1_rcv.at[part, i], line(axis, d), "line", part)

    g2t[...] = g2_ref[...].astype(F32).T.astype(BF16)
    outs.append(pltpu.make_async_copy(g2t, g2t_out, lsem.at[11]))
    outs[1].start()
    add_loss(2)
    spread_loss(3)

    for way, axis in enumerate((Y, Z)):
        for h in range(2):
            part = way + 2 * h
            total = hb[part, me[Y]] if axis == Y else hb[part, :, me[Z]]
            arrived(p1_rcv.at[part], "line", part)
            for i in range(3):
                total = total + p1_rcv[part, i].astype(F32)
            for q in range(4):
                for k in range(8):
                    p2_snd[way, q * 8 + k, :, h * 512 : (h + 1) * 512] = total[q, 2 * k : 2 * k + 2].astype(BF16)
        own = (me[Z] if axis == Y else me[Y]) * 8 + j_me
        p2_rcv[way, own] = p2_snd[way, own]
        for n in range(1, 32):
            to = rem(own + n, 32)
            q, k = div(to, 8), rem(to, 8)
            y, z = (me[Y], q) if axis == Y else (q, me[Z])
            send(
                p2_snd.at[way, to], p2_rcv.at[way, own], device(div(k, 2), y, z, rem(k, 2)), "direct", way
            )
    for way in range(2):
        arrived(p2_rcv.at[way, pl.ds(0, 31)], "direct", way)
    back = []
    for c in range(2):
        sums = []
        for way in range(2):
            total = jnp.zeros((2, 1024), F32)
            for k in range(16):
                total = total + p2_rcv[way, k * 2 + c].astype(F32)
            sums.append(total)
        for part in range(4):
            back.append(sums[part % 2][:, part // 2 * 512 : (part // 2 + 1) * 512])
    back = jnp.concatenate(back, axis=1) * sg[...].astype(F32).reshape(1, 4096)
    hat = s_ref[...].astype(F32) * stud_scale
    ig_ref[...] = stud_scale * (back - hat * jnp.mean(back * hat, axis=1, keepdims=True))
    add_loss(3)
    loss_ref[0, 0] = jnp.sum(jnp.where((sub == 0) & (lane == 0), ls_own[4], 0.0)) * (1.0 / 256)

    for out in outs:
        out.wait()
    left(s_snd.at[pl.ds(0, 7)], "spread")
    left(rows_a.at[0, pl.ds(0, 15)], "plane")
    left(rows_a.at[pl.ds(0, 3)], "ring")
    left(rows_a.at[pl.ds(0, 4)], "stud_side")
    left(gath.at[0, 0, pl.ds(0, 3), 0], "first")
    left(gath.at[0, pl.ds(0, 3), :, 0], "second")
    left(gath.at[pl.ds(0, 3), :, :, 0], "last")
    left(gath.at[:, :, :, 0], "side")
    left(st_rcv, "stats")
    left(ls_rcv.at[pl.ds(0, 10)], "loss")
    left(sib_snd, "sib")
    left(p1_snd.at[:, pl.ds(0, 3)], "line")
    left(p2_snd.at[:, pl.ds(0, 31)], "direct")
    for k, buf in enumerate((sl_snd, tl_snd, g_snd)):
        bulk_wait(buf, bulk_s, k)


def head_kernel(grad_hbm, rows_hbm, out_hbm, grad, rows, out, sems):
    load_grad = pltpu.make_async_copy(grad_hbm, grad, sems.at[16])
    load_grad.start()
    loads, stores = [], []
    for j in range(8):
        loads.append(pltpu.make_async_copy(rows_hbm.at[j], rows.at[j], sems.at[j]))
        loads[j].start()
    load_grad.wait()
    for j in range(8):
        cols = pl.ds(j * 512, 512)
        loads[j].wait()
        out[:, cols] = jnp.dot(
            grad[...], rows[j].reshape(256, 512), preferred_element_type=F32
        ).astype(BF16)
        stores.append(pltpu.make_async_copy(out.at[:, cols], out_hbm.at[:, cols], sems.at[8 + j]))
        stores[j].start()
    for store in stores:
        store.wait()


def body(
    teacher_hidden,
    teacher_gain,
    teacher_head,
    student_hidden,
    student_gain,
    student_head,
    token_ids,
    teacher_map,
    student_map,
):
    vmem = pl.BlockSpec(memory_space=pltpu.VMEM)
    hbm = pl.BlockSpec(memory_space=pltpu.HBM)
    loss, input_grad, grad, rows = pl.pallas_call(
        kernel,
        out_shape=(
            jax.ShapeDtypeStruct((1, 1), F32),
            jax.ShapeDtypeStruct((2, 4096), F32),
            jax.ShapeDtypeStruct((512, 256), BF16),
            jax.ShapeDtypeStruct((8, 16, 16, 512), BF16),
        ),
        in_specs=[hbm] * 9,
        out_specs=(pl.BlockSpec(memory_space=pltpu.SMEM), vmem, hbm, hbm),
        scratch_shapes=[
            pltpu.VMEM((4, 4, 4, 2, 128, 256), BF16),
            pltpu.VMEM((512, 16384), BF16),
            pltpu.VMEM((512, 4096), BF16),
            pltpu.VMEM((16384,), BF16),
            pltpu.VMEM((4096,), BF16),
            pltpu.VMEM((2, 4096), BF16),
            pltpu.VMEM((128,), jnp.int32),
            pltpu.VMEM((128,), jnp.int32),
            pltpu.VMEM((8, 128), jnp.int32),
            pltpu.SMEM((256,), jnp.int32),
            pltpu.SMEM((8, 128), jnp.int32),
            pltpu.VMEM((256, 512), F32),
            pltpu.VMEM((256, 512), F32),
            pltpu.VMEM((8, 16, 16, 512), BF16),
            pltpu.VMEM((8, 2, 512), BF16),
            pltpu.VMEM((8, 2, 512), BF16),
            pltpu.VMEM((5, 2, 8, 128), F32),
            pltpu.VMEM((10, 2, 8, 128), F32),
            pltpu.VMEM((2, 128, 128), F32),
            pltpu.VMEM((128, 8, 128), BF16),
            pltpu.VMEM((128, 8, 128), BF16),
            pltpu.VMEM((128, 8, 128), BF16),
            pltpu.VMEM((128, 8, 128), BF16),
            pltpu.VMEM((128, 8, 128), BF16),
            pltpu.VMEM((128, 8, 128), BF16),
            pltpu.VMEM((256, 512), BF16),
            pltpu.VMEM((512, 256), BF16),
            pltpu.VMEM((4, 4, 4, 16, 512), BF16),
            pltpu.VMEM((4, 4, 4, 16, 512), BF16),
            pltpu.VMEM((4, 4, 4, 16, 512), F32),
            pltpu.VMEM((4, 4, 4, 16, 512), BF16),
            pltpu.VMEM((4, 3, 4, 16, 512), BF16),
            pltpu.VMEM((2, 32, 2, 1024), BF16),
            pltpu.VMEM((2, 32, 2, 1024), BF16),
            pltpu.VMEM((5, 8, 128), F32),
            pltpu.VMEM((13, 8, 128), F32),
            pltpu.SemaphoreType.DMA((len(SEND),)),
            pltpu.SemaphoreType.DMA((N_RECV,)),
            pltpu.SemaphoreType.DMA((12,)),
            pltpu.SemaphoreType.DMA((3,)),
            pltpu.SemaphoreType.DMA((3,)),
        ],
        compiler_params=pltpu.CompilerParams(
            collective_id=0, has_side_effects=True, vmem_limit_bytes=63 << 20
        ),
        cost_estimate=pl.CostEstimate(
            flops=2 * 256 * 512 * (16384 + 3 * 4096), bytes_accessed=24 << 20, transcendentals=0
        ),
        name="distill",
    )(
        teacher_hidden,
        teacher_gain,
        teacher_head,
        student_hidden,
        student_gain,
        student_head,
        token_ids,
        teacher_map,
        student_map,
    )
    head_grad = pl.pallas_call(
        head_kernel,
        out_shape=jax.ShapeDtypeStruct((512, 4096), BF16),
        in_specs=[hbm, hbm],
        out_specs=hbm,
        scratch_shapes=[
            pltpu.VMEM((512, 256), BF16),
            pltpu.VMEM((8, 16, 16, 512), BF16),
            pltpu.VMEM((512, 4096), BF16),
            pltpu.SemaphoreType.DMA((17,)),
        ],
        compiler_params=pltpu.CompilerParams(vmem_limit_bytes=63 << 20),
        cost_estimate=pl.CostEstimate(
            flops=2 * 256 * 512 * 4096, bytes_accessed=6 << 20, transcendentals=0
        ),
        name="head",
    )(grad, rows)
    return (loss.reshape(()), head_grad, input_grad)


def solution(mesh):
    placed = (
        P("role", "vocab"),
        P(),
        P(("role", "vocab"), None),
        P(("role", "vocab"), None),
        P(),
        P(("role", "vocab"), None),
        P(),
        P(),
        P(),
    )
    return jax.shard_map(
        body,
        mesh=mesh,
        in_specs=placed,
        out_specs=(P(), P(("role", "vocab"), None), P(("role", "vocab"), None)),
        check_vma=False,
    )
```

time: 109 us -> 94.1 us (0.86)
  other arithmetic: 5.44 us -> 0 us
  matrix products: 4.98 us -> 0 us
  Pallas kernels: 94.4 us -> 90.8 us
  local copies, waits for them, and re-layouts: 3.22 us -> 0.62 us
  between operations: 0.65 us -> 2.47 us
    dot_general x1 -> x0, matrix products: 4.98 us -> none  [body(): lax.dot_general(grad, rows.reshape(256, 4096), (((0,), (0,)), ((), ())),...]
    pallas_call x1 -> x2, Pallas kernels: 94.4 us -> 90.8 us  [the longest x1 86.4 us: body(): pl.pallas_call(kernel, out_shape=(jax.ShapeDtypeStruct((1, 1), F32), jax....]
    reduce_sum x2 -> x0, other arithmetic: 2.19 us -> none  [positions(): jnp.sum(jnp.where(match, jnp.arange(count, dtype=jnp.int32)[None, :], 0),...]
    reshape x1 -> x0, local copies, waits for them, and re-layouts: 1.4 us -> none  [body(): teacher_gain.astype(F32).reshape(16, 1024)]
    reshape x1 -> x0, other arithmetic: 1.3 us -> none  [body(): student_gain.astype(F32).reshape(1, 4096)]
    add x1 -> x0, other arithmetic: 1.26 us -> none  [body(): label_col = positions(student_map, token_ids // 512) * 512 + token_ids % 512]
    slice x1 -> x0, local copies, waits for them, and re-layouts: 1.2 us -> none  [body(): return (loss[0, 0], head_grad, input_grad)]
where the time goes in v2:
time: 94.1 us; the launch traced here: 93.9 us
  Pallas kernels  90.8 us (96%)
  between operations  2.47 us (3%)
    pallas_call x1, Pallas kernels, body(): pl.pallas_call(kernel, out_shape=(jax.ShapeDtypeStruct((1, 1), F32), jax....  86.4 us
    pallas_call x1, Pallas kernels, body(): pl.pallas_call(head_kernel, out_shape=jax.ShapeDtypeStruct((512, 4096), B...  4.4 us

profile of v2, /device:TPU:1, one launch (start us, length us, event | category | flops | bytes accessed | tf_op | source)
XLA Modules:
  0.0 93.9 jit_solution(3135329330449254003)
XLA Ops:
  0.6 86.4 %distill.1 = (f32[1,1]{1,0:T(1,128)}, f32[2,4096]{1,0:T(2,128)}, bf16[512,256]{1,0:T(8,128)(2,1)}, bf16[8,16,16,512]{3,2,1,0:T(8,128)(2,1)}) custom-call(bf16[128,256]{1,0:T(8,128)(2,1)} %t_hbm.1, bf16[16384]{0:T(1024)(128)(2,1)} %tg_hbm.1, bf16[512,16384]{1,0:T(8,128)(2,1)} %th_hbm.1, bf16[2,4096]{1,0:T(2,128)(2,1)} %s_hbm.1, bf16[4096]{0:T(1024)(128)(2,1)} %sg_hbm.1, ...), custom_call_target="tpu_custom_call" | custom-call | flops 7516192768 | bytes 25165824 | tf_op jit(solution)/shard_map/distill/pallas_call | solution.py:693
  87.0 0.0 copy-start
  87.1 4.4 %head.1 = bf16[512,4096]{1,0:T(8,128)(2,1)} custom-call(bf16[512,256]{1,0:T(8,128)(2,1)} %get-tuple-element.8.grad_hbm, bf16[8,16,16,512]{3,2,1,0:T(8,128)(2,1)} %get-tuple-element.9.rows_hbm), custom_call_target="tpu_custom_call" | custom-call | flops 1073741824 | bytes 6291456 | tf_op jit(solution)/shard_map/head/pallas_call | solution.py:764
  92.1 0.0 copy-done
  92.1 0.6 copy.15
Async XLA Ops:
  87.0 5.1 %copy-start = (f32[2,4096]{1,0:T(2,128)S(1)}, f32[2,4096]{1,0:T(2,128)}, u32[]{:S(2)}) copy-start(f32[2,4096]{1,0:T(2,128)} %get-tuple-element.16) | copy-start | bytes 98308

commit v3 on v2

--- a/solution.py
+++ b/solution.py
@@ -186,6 +186,11 @@
         s_snd[j] = stud_normed[:, j * 512 : (j + 1) * 512]
     s_rcv[j_me] = s_snd[j_me]
     loads[0].wait()
+    own_f = own_slot[...].astype(F32)
+    sums = jnp.sum(own_f * own_f, axis=1, keepdims=True)
+    flipped = jnp.broadcast_to(sums, (128, 128)).T[:8]
+    st_own[0, 0] = jnp.where(role == 0, flipped, 0.0)
+    st_own[0, 1] = jnp.where(role == 1, flipped, 0.0)
 
     pl.semaphore_wait(barrier, 22)
 
@@ -225,12 +230,6 @@
             send(mine(p), mine(p), line(c, d), "heavy", last_no(p, 0, d), "last")
         for d in steps:
             send(mine(p), mine(p), line(b, d), "second", no(p, d))
-    own_f = own_slot[...].astype(F32)
-    sums = jnp.sum(own_f * own_f, axis=1, keepdims=True)
-    flipped = jnp.broadcast_to(sums, (128, 128)).T[:8]
-    st_own[0, 0] = jnp.where(role == 0, flipped, 0.0)
-    st_own[0, 1] = jnp.where(role == 1, flipped, 0.0)
-
     def spread_stats(stage):
         for i, d in enumerate(steps):
             send(st_own.at[stage], st_rcv.at[stage * 3 + i], line((X, Y, Z)[stage], d), "stats", stage)
@@ -269,8 +268,6 @@
                 send(block, block, line(b, e), "second", no(p, e))
             for e in (1, 3):
                 send(block, block, line(c, e), "heavy", last_no(p, 0, e), "last")
-    add_stats(0)
-    spread_stats(1)
     for p in parts:
         a, b, c = axes(p)
         to_side(0, at(p, ALL, me[b], me[c]))
@@ -285,6 +282,8 @@
     for d, half, n in ways:
         send(chunk(0, half), chunk(0, half), line(X, d), "ring", n)
     to_stud_side(chunk(0))
+    add_stats(0)
+    spread_stats(1)
 
     for g, d in enumerate(steps):
         for p in parts:
@@ -294,9 +293,6 @@
             for e in (1, 3):
                 send(group, group, line(c, e), "heavy", last_no(p, g + 1, e), "last")
             to_side(g + 1, group)
-    add_stats(1)
-    spread_stats(2)
-
     for load in loads[7:]:
         load.start()
 
@@ -312,8 +308,8 @@
 
     two = ((1, pl.ds(0, 2)), (3, pl.ds(2, 2)))
 
-    def pass_heavy(g):
-        for p in parts:
+    def pass_heavy(g, which=parts):
+        for p in which:
             c = axes(p)[2]
             for d, half in two:
                 from_c = moved(c, 4 - d)
@@ -331,8 +327,8 @@
             to_side(g, group)
 
     pass_heavy(0)
-    add_stats(2)
-    send(st_own.at[3], st_rcv.at[9], sibling, "stats", 3)
+    add_stats(1)
+    spread_stats(2)
     for d, half, n in ways[:2]:
         piece = chunk(4 - d, half)
         arrived(piece, "ring", n)
@@ -346,11 +342,8 @@
     pass_halves(0)
     arrived(chunk(2), "far")
     to_stud_side(chunk(2))
-    arrived(st_rcv.at[9], "stats", 3)
-    for r in range(2):
-        total = st_own[3, r] + st_rcv[9, r]
-        scale = lax.rsqrt(total * (1.0 / 16384) + EPS)
-        scale_ref[r] = jnp.broadcast_to(scale[0:1], (128, 128)).T
+    add_stats(2)
+    send(st_own.at[3], st_rcv.at[9], sibling, "stats", 3)
     pass_heavy(2)
     pass_halves(1)
 
@@ -358,35 +351,36 @@
     lane = lax.broadcasted_iota(jnp.int32, (8, 128), 1)
     pair = sub // 2
 
-    def start_bulk(src, dst, to, sem):
-        pltpu.make_async_remote_copy(
-            src,
-            dst,
-            bulk_s.at[sem],
-            bulk_r.at[sem],
-            device_id=(div(to, 64), rem(to, 64)),
-            device_id_type=MESH,
-        ).start()
-
-    def fill_messages(source, out, r, index):
+    def fill_messages(source, which, r, index):
         rows = source[pl.ds(pl.multiple_of(r * 8, 8), 8), :]
         tiles = shuffle4([rows[:, j * 128 : (j + 1) * 128] for j in range(4)], pair)
         for k in range(4):
-            out[index(r, jnp.int32(k))] = tiles[k].astype(BF16)
-
-    def to_owners(source, out, into, own_r, own_k, index, sem, i):
-        r = rem(own_r + i, 32)
-        fill_messages(source, out, r, index)
-        for k in range(4):
-            to = index(r, jnp.int32(k))
-            start_bulk(out.at[to], into.at[flat], to, sem)
-
-    def to_near_owners(source, out, into, own_r, own_k, index, sem):
-        fill_messages(source, out, own_r, index)
-        into[flat] = out[flat]
-        for i in range(1, 4):
-            to = index(own_r, rem(own_k + i, 4))
-            start_bulk(out.at[to], into.at[flat], to, sem)
+            which[index(r, jnp.int32(k))] = tiles[k].astype(BF16)
+
+    role_at = [div(moved(Y, b), 2) for b in range(4)]
+    y_at = [rem(moved(Y, b), 2) * 8 for b in range(4)]
+    x_at = [moved(X, a) * 16 for a in range(4)]
+    z_at = [moved(Z, c) * 2 for c in range(4)]
+    c_at = [me_c, 1 - me_c]
+    near_last = sorted(
+        ((a, c, e) for a in range(4) for c in range(4) for e in range(2)),
+        key=lambda place: (-min(place[0], 4 - place[0]) - min(place[1], 4 - place[1]), -place[2]),
+    )
+
+    def send_plane(snd, rcv, sem, b):
+        for a, c, e in near_last:
+            if (a, b, c, e) != (0, 0, 0, 0):
+                vocab_to = x_at[a] + y_at[b] + z_at[c] + c_at[e]
+                pltpu.make_async_remote_copy(
+                    snd.at[role_at[b] * 64 + vocab_to],
+                    rcv.at[flat],
+                    bulk_s.at[sem],
+                    bulk_r.at[sem],
+                    device_id=(role_at[b], vocab_to),
+                    device_id_type=MESH,
+                ).start()
+
+    planes = (2, 1, 3, 0)
 
     def column_index(r, k):
         g = div(r, 2)
@@ -411,11 +405,25 @@
             acc_s[...] = part
         else:
             acc_s[...] += part
-    stud_args = (acc_s, sl_snd, sl_rcv, g_me * 2 + div(me[X], 2), rem(me[X], 2) * 2 + me_c, column_index, 0)
-    pass_heavy(3)
+
+    @pl.loop(0, 32, unroll=4)
+    def _(r):
+        fill_messages(acc_s, sl_snd, r, column_index)
+
+    sl_rcv[flat] = sl_snd[flat]
+
+    for p in parts:
+        send_plane(sl_snd, sl_rcv, 0, planes[p])
+        pass_heavy(3, (p,))
+    send_plane(sl_snd, sl_rcv, 0, 0)
     pass_halves(2)
     outs = [pltpu.make_async_copy(rows_a, rows_out, lsem.at[10])]
     outs[0].start()
+    arrived(st_rcv.at[9], "stats", 3)
+    for r in range(2):
+        total = st_own[3, r] + st_rcv[9, r]
+        scale = lax.rsqrt(total * (1.0 / 16384) + EPS)
+        scale_ref[r] = jnp.broadcast_to(scale[0:1], (128, 128)).T
 
     load_th.wait()
     arrived(gath.at[pl.ds(0, 3), :, :, 0], "side", 0)
@@ -423,11 +431,11 @@
 
     def teacher_step(dx, dz):
         x, z = rem(me[X] + dx, 4), rem(me[Z] + dz, 4)
-        total = None
+        lanes, heads = [], []
         for y_lo in range(2):
             base = pl.multiple_of(x * 4096 + y_lo * 2048 + z * 512, 512)
             gain = tg[pl.ds(base, 512)].astype(F32).reshape(1, 512)
-            lanes = []
+            heads.append(th[:, pl.ds(base, 512)])
             for c in range(2):
                 rows = []
                 for r in range(2):
@@ -436,29 +444,20 @@
                     scale = jnp.concatenate([scale, scale], axis=1)
                     rows.append((block * scale * gain[:, c * 256 : (c + 1) * 256]).astype(BF16))
                 lanes.append(jnp.concatenate(rows, axis=0))
-            part = lax.dot_general(
-                jnp.concatenate(lanes, axis=1),
-                th[:, pl.ds(base, 512)],
-                (((1,), (1,)), ((), ())),
-                preferred_element_type=F32,
-            )
-            total = part if total is None else total + part
-        acc[...] += total
+        acc[...] += lax.dot_general(
+            jnp.concatenate(lanes, axis=1),
+            jnp.concatenate(heads, axis=1),
+            (((1,), (1,)), ((), ())),
+            preferred_element_type=F32,
+        )
 
     @pl.loop(0, 9)
     def _(i):
         q, w = div(i, 3), rem(i, 3)
-        for n in range(1, 4):
-            to_owners(*stud_args, i * 3 + n)
         teacher_step(q + div(q, 2), w + div(w, 2))
 
     pass_halves(3)
 
-    @pl.loop(28, 32)
-    def _(i):
-        to_owners(*stud_args, i)
-
-    to_near_owners(*stud_args)
     arrived(gath.at[0, :, :, 0], "side", 1)
 
     @pl.loop(0, 4)
@@ -469,13 +468,15 @@
     def _(q):
         teacher_step(q + div(q, 2), 2)
 
-    teach_args = (acc, tl_snd, tl_rcv, div(flat, 4), rem(flat, 4), plain_index, 1)
-
-    @pl.loop(1, 32)
-    def _(i):
-        to_owners(*teach_args, i)
-
-    to_near_owners(*teach_args)
+    for b in planes:
+        base = role_at[b] * 16 + div(y_at[b], 4)
+
+        @pl.loop(0, 8, unroll=4)
+        def _(i, base=base):
+            fill_messages(acc, tl_snd, base + i + 2 * div(i, 2), plain_index)
+
+        send_plane(tl_snd, tl_rcv, 1, b)
+    tl_rcv[flat] = tl_snd[flat]
 
     def over(value, op, reduce):
         value = jnp.broadcast_to(reduce(value, axis=1, keepdims=True), (8, 128))
@@ -490,7 +491,8 @@
         top = over(top, jnp.maximum, jnp.max)
 
         def sum_step(i, total):
-            return total + jnp.sum(jnp.exp(ref[pl.ds(i * 16, 16)].astype(F32) - top[None]), axis=0)
+            part = jnp.exp(ref[pl.ds(i * 16, 16)].astype(F32) - top[None])
+            return total + jnp.sum(part, axis=0)
 
         total = lax.fori_loop(0, 8, sum_step, jnp.zeros((8, 128), F32))
         return top + jnp.log(over(total, jnp.add, jnp.sum))
@@ -512,8 +514,7 @@
     wanted = jnp.where(token == 0, label_place(ids[flat * 2]), label_place(ids[flat * 2 + 1]))
     place = pair * 128 + lane
 
-    def term(n, carry):
-        i = rem(n + flat, 128)
+    def term(i, carry):
         teach = tl_rcv[jnp.clip(order_ref[0, i], 0, 127)].astype(F32)
         student = sl_rcv[i].astype(F32)
         teach_prob = jnp.exp(teach - teach_log)
@@ -525,15 +526,13 @@
         g_snd[i] = grad.astype(BF16)
         return carry + teach_prob * (teach - student) - CE_WEIGHT * jnp.where(hit, student, 0.0)
 
-    def term_and_send(n, carry):
-        carry = term(n, carry)
-        i = rem(n + flat, 128)
-        start_bulk(g_snd.at[i], g_rcv.at[flat], i, 2)
-        return carry
-
-    total = lax.fori_loop(1, 127, term_and_send, jnp.zeros((8, 128), F32), unroll=6)
-    total = term_and_send(jnp.int32(127), total)
-    total = term(jnp.int32(0), total)
+    total = jnp.zeros((8, 128), F32)
+    for b in planes:
+        base = role_at[b] * 64 + y_at[b]
+        total = lax.fori_loop(
+            0, 32, lambda j, carry, base=base: term(base + j + 8 * div(j, 8), carry), total, unroll=8
+        )
+        send_plane(g_snd, g_rcv, 2, b)
     g_rcv[flat] = g_snd[flat]
     once = (sub < 2) & (lane == 0)
     total = total + jnp.where(once, (1.0 + CE_WEIGHT) * stud_log - teach_log, 0.0)
@@ -613,12 +612,15 @@
                     p2_snd[way, q * 8 + k, :, h * 512 : (h + 1) * 512] = total[q, 2 * k : 2 * k + 2].astype(BF16)
         own = (me[Z] if axis == Y else me[Y]) * 8 + j_me
         p2_rcv[way, own] = p2_snd[way, own]
-        for n in range(1, 32):
-            to = rem(own + n, 32)
-            q, k = div(to, 8), rem(to, 8)
+        other = Z if axis == Y else Y
+        for a, o, e in near_last:
+            if (a, o, e) == (0, 0, 0):
+                continue
+            q, x, c = moved(other, o), moved(X, a), c_at[e]
+            to = q * 8 + x * 2 + c
             y, z = (me[Y], q) if axis == Y else (q, me[Z])
             send(
-                p2_snd.at[way, to], p2_rcv.at[way, own], device(div(k, 2), y, z, rem(k, 2)), "direct", way
+                p2_snd.at[way, to], p2_rcv.at[way, own], device(x, y, z, c), "direct", way
             )
     for way in range(2):
         arrived(p2_rcv.at[way, pl.ds(0, 31)], "direct", way)
@@ -657,7 +659,9 @@
         bulk_wait(buf, bulk_s, k)
 
 
-def head_kernel(grad_hbm, rows_hbm, out_hbm, grad, rows, out, sems):
+def head_kernel(grad_hbm, rows_hbm, ig_hbm, out_hbm, ig_out, grad, rows, out, sems):
+    move_ig = pltpu.make_async_copy(ig_hbm, ig_out, sems.at[17])
+    move_ig.start()
     load_grad = pltpu.make_async_copy(grad_hbm, grad, sems.at[16])
     load_grad.start()
     loads, stores = [], []
@@ -675,6 +679,7 @@
         stores[j].start()
     for store in stores:
         store.wait()
+    move_ig.wait()
 
 
 def body(
@@ -761,23 +766,26 @@
         teacher_map,
         student_map,
     )
-    head_grad = pl.pallas_call(
+    head_grad, input_grad = pl.pallas_call(
         head_kernel,
-        out_shape=jax.ShapeDtypeStruct((512, 4096), BF16),
-        in_specs=[hbm, hbm],
-        out_specs=hbm,
+        out_shape=(
+            jax.ShapeDtypeStruct((512, 4096), BF16),
+            jax.ShapeDtypeStruct((2, 4096), F32),
+        ),
+        in_specs=[hbm, hbm, hbm],
+        out_specs=(hbm, hbm),
         scratch_shapes=[
             pltpu.VMEM((512, 256), BF16),
             pltpu.VMEM((8, 16, 16, 512), BF16),
             pltpu.VMEM((512, 4096), BF16),
-            pltpu.SemaphoreType.DMA((17,)),
+            pltpu.SemaphoreType.DMA((18,)),
         ],
         compiler_params=pltpu.CompilerParams(vmem_limit_bytes=63 << 20),
         cost_estimate=pl.CostEstimate(
             flops=2 * 256 * 512 * 4096, bytes_accessed=6 << 20, transcendentals=0
         ),
         name="head",
-    )(grad, rows)
+    )(grad, rows, input_grad)
     return (loss.reshape(()), head_grad, input_grad)
 
 

time: 94.1 us -> 89 us (0.946)
  Pallas kernels: 90.8 us -> 86.4 us
    pallas_call x1, Pallas kernels: 86.4 us -> 82 us  [body(): pl.pallas_call(kernel, out_shape=(jax.ShapeDtypeStruct((1, 1), F32), jax....]
where the time goes in v3:
time: 89 us; the launch traced here: 88.8 us
  Pallas kernels  86.4 us (97%)
  between operations  2.45 us (3%)
    pallas_call x1, Pallas kernels, body(): pl.pallas_call(kernel, out_shape=(jax.ShapeDtypeStruct((1, 1), F32), jax....  82 us
    pallas_call x1, Pallas kernels, body(): pl.pallas_call(head_kernel, out_shape=(jax.ShapeDtypeStruct((512, 4096),...  4.4 us

profile of v3, /device:TPU:1, one launch (start us, length us, event | category | flops | bytes accessed | tf_op | source)
XLA Modules:
  0.0 88.8 jit_solution(4400849735897761256)
XLA Ops:
  0.6 82.0 %distill.1 = (f32[1,1]{1,0:T(1,128)}, f32[2,4096]{1,0:T(2,128)}, bf16[512,256]{1,0:T(8,128)(2,1)}, bf16[8,16,16,512]{3,2,1,0:T(8,128)(2,1)}) custom-call(bf16[128,256]{1,0:T(8,128)(2,1)} %t_hbm.1, bf16[16384]{0:T(1024)(128)(2,1)} %tg_hbm.1, bf16[512,16384]{1,0:T(8,128)(2,1)} %th_hbm.1, bf16[2,4096]{1,0:T(2,128)(2,1)} %s_hbm.1, bf16[4096]{0:T(1024)(128)(2,1)} %sg_hbm.1, ...), custom_call_target="tpu_custom_call" | custom-call | flops 7516192768 | bytes 25165824 | tf_op jit(solution)/shard_map/distill/pallas_call | solution.py:698
  82.6 4.4 %head.1 = (bf16[512,4096]{1,0:T(8,128)(2,1)}, f32[2,4096]{1,0:T(2,128)}) custom-call(bf16[512,256]{1,0:T(8,128)(2,1)} %get-tuple-element.10.grad_hbm, bf16[8,16,16,512]{3,2,1,0:T(8,128)(2,1)} %get-tuple-element.11.rows_hbm, f32[2,4096]{1,0:T(2,128)} %get-tuple-element.12.ig_hbm), custom_call_target="tpu_custom_call" | custom-call | flops 1073741824 | bytes 6291456 | tf_op jit(solution)/shard_map/head/pallas_call | solution.py:769

commit v4 on v3

--- a/solution.py
+++ b/solution.py
@@ -19,7 +19,7 @@
 )}
 RECV_COUNTS = dict(
     spread=1, plane=1, ring=4, far=1, stud_side=1, first=9, second=9, heavy=24, halves=12,
-    side=2, stats=4, loss=4, sib=4, line=4, direct=2,
+    side=3, stats=4, loss=4, sib=4, line=4, direct=2,
 )
 RECV = {name: sum(list(RECV_COUNTS.values())[:k]) for k, name in enumerate(RECV_COUNTS)}
 N_RECV = sum(RECV_COUNTS.values())
@@ -244,7 +244,7 @@
     spread_stats(0)
 
     def to_side(g, ref):
-        send(ref, ref, sibling, "side", g // 3)
+        send(ref, ref, sibling, "side", max(g - 1, 0))
 
     def to_stud_side(ref):
         send(ref, ref, sibling, "stud_side")
@@ -392,41 +392,12 @@
     def bulk_wait(buf, sems, sem):
         pltpu.make_async_copy(buf.at[pl.ds(0, 127)], buf.at[pl.ds(0, 127)], sems.at[sem]).wait()
 
-    arrived(rows_a.at[pl.ds(0, 4)], "stud_side")
-    load_sh.wait()
-    for j in range(8):
-        part = lax.dot_general(
-            rows_a[j].reshape(256, 512),
-            sh[:, j * 512 : (j + 1) * 512],
-            (((1,), (1,)), ((), ())),
-            preferred_element_type=F32,
-        )
-        if j == 0:
-            acc_s[...] = part
-        else:
-            acc_s[...] += part
-
-    @pl.loop(0, 32, unroll=4)
-    def _(r):
-        fill_messages(acc_s, sl_snd, r, column_index)
-
-    sl_rcv[flat] = sl_snd[flat]
-
-    for p in parts:
-        send_plane(sl_snd, sl_rcv, 0, planes[p])
-        pass_heavy(3, (p,))
-    send_plane(sl_snd, sl_rcv, 0, 0)
-    pass_halves(2)
-    outs = [pltpu.make_async_copy(rows_a, rows_out, lsem.at[10])]
-    outs[0].start()
     arrived(st_rcv.at[9], "stats", 3)
     for r in range(2):
         total = st_own[3, r] + st_rcv[9, r]
         scale = lax.rsqrt(total * (1.0 / 16384) + EPS)
         scale_ref[r] = jnp.broadcast_to(scale[0:1], (128, 128)).T
-
     load_th.wait()
-    arrived(gath.at[pl.ds(0, 3), :, :, 0], "side", 0)
     acc[...] = jnp.zeros_like(acc)
 
     def teacher_step(dx, dz):
@@ -451,14 +422,52 @@
             preferred_element_type=F32,
         )
 
-    @pl.loop(0, 9)
+    arrived(gath.at[pl.ds(0, 2), :, :, 0], "side", 0)
+
+    @pl.loop(0, 4)
     def _(i):
-        q, w = div(i, 3), rem(i, 3)
-        teacher_step(q + div(q, 2), w + div(w, 2))
-
+        teacher_step(3 * div(i, 2), 3 * rem(i, 2))
+
+    pass_heavy(3)
+    pass_halves(2)
+
+    arrived(rows_a.at[pl.ds(0, 4)], "stud_side")
+    load_sh.wait()
+    for j in range(8):
+        part = lax.dot_general(
+            rows_a[j].reshape(256, 512),
+            sh[:, j * 512 : (j + 1) * 512],
+            (((1,), (1,)), ((), ())),
+            preferred_element_type=F32,
+        )
+        if j == 0:
+            acc_s[...] = part
+        else:
+            acc_s[...] += part
+
+    @pl.loop(0, 32, unroll=4)
+    def _(r):
+        fill_messages(acc_s, sl_snd, r, column_index)
+
+    sl_rcv[flat] = sl_snd[flat]
+
+    for b in planes:
+        send_plane(sl_snd, sl_rcv, 0, b)
     pass_halves(3)
+    outs = [pltpu.make_async_copy(rows_a, rows_out, lsem.at[10])]
+    outs[0].start()
 
     arrived(gath.at[0, :, :, 0], "side", 1)
+
+    @pl.loop(0, 2)
+    def _(i):
+        teacher_step(3 * i, 1)
+
+    @pl.loop(0, 3)
+    def _(i):
+        teacher_step(1, i + div(i, 2))
+
+    arrived(gath.at[0, :, :, 0], "side", 2)
 
     @pl.loop(0, 4)
     def _(i):

time: 89 us -> 87.8 us (0.987)
  Pallas kernels: 86.4 us -> 85.2 us
    pallas_call x1, Pallas kernels: 82 us -> 80.8 us  [body(): pl.pallas_call(kernel, out_shape=(jax.ShapeDtypeStruct((1, 1), F32), jax....]
where the time goes in v4:
time: 87.8 us; the launch traced here: 87.7 us
  Pallas kernels  85.2 us (97%)
  between operations  2.45 us (3%)
    pallas_call x1, Pallas kernels, body(): pl.pallas_call(kernel, out_shape=(jax.ShapeDtypeStruct((1, 1), F32), jax....  80.8 us
    pallas_call x1, Pallas kernels, body(): pl.pallas_call(head_kernel, out_shape=(jax.ShapeDtypeStruct((512, 4096),...  4.39 us

profile of v4, /device:TPU:1, one launch (start us, length us, event | category | flops | bytes accessed | tf_op | source)
XLA Modules:
  0.0 87.7 jit_solution(13751574201634886569)
XLA Ops:
  0.6 80.8 %distill.1 = (f32[1,1]{1,0:T(1,128)}, f32[2,4096]{1,0:T(2,128)}, bf16[512,256]{1,0:T(8,128)(2,1)}, bf16[8,16,16,512]{3,2,1,0:T(8,128)(2,1)}) custom-call(bf16[128,256]{1,0:T(8,128)(2,1)} %t_hbm.1, bf16[16384]{0:T(1024)(128)(2,1)} %tg_hbm.1, bf16[512,16384]{1,0:T(8,128)(2,1)} %th_hbm.1, bf16[2,4096]{1,0:T(2,128)(2,1)} %s_hbm.1, bf16[4096]{0:T(1024)(128)(2,1)} %sg_hbm.1, ...), custom_call_target="tpu_custom_call" | custom-call | flops 7516192768 | bytes 25165824 | tf_op jit(solution)/shard_map/distill/pallas_call | solution.py:707
  81.5 4.4 %head.1 = (bf16[512,4096]{1,0:T(8,128)(2,1)}, f32[2,4096]{1,0:T(2,128)}) custom-call(bf16[512,256]{1,0:T(8,128)(2,1)} %get-tuple-element.10.grad_hbm, bf16[8,16,16,512]{3,2,1,0:T(8,128)(2,1)} %get-tuple-element.11.rows_hbm, f32[2,4096]{1,0:T(2,128)} %get-tuple-element.12.ig_hbm), custom_call_target="tpu_custom_call" | custom-call | flops 1073741824 | bytes 6291456 | tf_op jit(solution)/shard_map/head/pallas_call | solution.py:778

commit v5 on v4

--- a/solution.py
+++ b/solution.py
@@ -18,7 +18,7 @@
     ("spread", "plane", "ring", "stud_side", "first", "second", "last", "side", "stats", "loss", "sib", "line", "direct")
 )}
 RECV_COUNTS = dict(
-    spread=1, plane=1, ring=4, far=1, stud_side=1, first=9, second=9, heavy=24, halves=12,
+    spread=1, plane=1, ring=4, far=1, stud_side=1, first=9, second=9, heavy=24, halves=4,
     side=3, stats=4, loss=4, sib=4, line=4, direct=2,
 )
 RECV = {name: sum(list(RECV_COUNTS.values())[:k]) for k, name in enumerate(RECV_COUNTS)}
@@ -316,15 +316,13 @@
                 group = at(p, ALL, offset_b(p, g), from_c)
                 arrived(group, "heavy", last_no(p, g, d))
                 piece = at(p, half, offset_b(p, g), from_c)
-                send(piece, piece, line(c, d), "halves", p * 4 + g, "last")
+                send(piece, piece, line(c, d), "halves", g, "last")
                 to_side(g, group)
 
     def pass_halves(g):
+        arrived(gath.at[0, 0, :, 0], "halves", g)
         for p in parts:
-            c = axes(p)[2]
-            group = at(p, ALL, offset_b(p, g), moved(c, 2))
-            arrived(group, "halves", p * 4 + g)
-            to_side(g, group)
+            to_side(g, at(p, ALL, offset_b(p, g), moved(axes(p)[2], 2)))
 
     pass_heavy(0)
     add_stats(1)
@@ -400,10 +398,11 @@
     load_th.wait()
     acc[...] = jnp.zeros_like(acc)
 
-    def teacher_step(dx, dz):
-        x, z = rem(me[X] + dx, 4), rem(me[Z] + dz, 4)
+    def teacher_step(*places):
         lanes, heads = [], []
-        for y_lo in range(2):
+        for x, z, y_lo in (
+            (rem(me[X] + dx, 4), rem(me[Z] + dz, 4), y_lo) for dx, dz in places for y_lo in range(2)
+        ):
             base = pl.multiple_of(x * 4096 + y_lo * 2048 + z * 512, 512)
             gain = tg[pl.ds(base, 512)].astype(F32).reshape(1, 512)
             heads.append(th[:, pl.ds(base, 512)])
@@ -424,19 +423,19 @@
 
     arrived(gath.at[pl.ds(0, 2), :, :, 0], "side", 0)
 
-    @pl.loop(0, 4)
+    @pl.loop(0, 2)
     def _(i):
-        teacher_step(3 * div(i, 2), 3 * rem(i, 2))
+        teacher_step((3 * i, 0), (3 * i, 3))
 
     pass_heavy(3)
     pass_halves(2)
 
     arrived(rows_a.at[pl.ds(0, 4)], "stud_side")
     load_sh.wait()
-    for j in range(8):
+    for j in range(2):
         part = lax.dot_general(
-            rows_a[j].reshape(256, 512),
-            sh[:, j * 512 : (j + 1) * 512],
+            jnp.concatenate([rows_a[4 * j + k].reshape(256, 512) for k in range(4)], axis=1),
+            sh[:, j * 2048 : (j + 1) * 2048],
             (((1,), (1,)), ((), ())),
             preferred_element_type=F32,
         )
@@ -445,7 +444,7 @@
         else:
             acc_s[...] += part
 
-    @pl.loop(0, 32, unroll=4)
+    @pl.loop(0, 32, unroll=8)
     def _(r):
         fill_messages(acc_s, sl_snd, r, column_index)
 
@@ -459,28 +458,21 @@
 
     arrived(gath.at[0, :, :, 0], "side", 1)
 
+    teacher_step((0, 1), (3, 1))
+    teacher_step((1, 0), (1, 1), (1, 3))
+
+    arrived(gath.at[0, :, :, 0], "side", 2)
+
     @pl.loop(0, 2)
     def _(i):
-        teacher_step(3 * i, 1)
-
-    @pl.loop(0, 3)
-    def _(i):
-        teacher_step(1, i + div(i, 2))
-
-    arrived(gath.at[0, :, :, 0], "side", 2)
-
-    @pl.loop(0, 4)
-    def _(i):
-        teacher_step(2, i)
-
-    @pl.loop(0, 3)
-    def _(q):
-        teacher_step(q + div(q, 2), 2)
+        teacher_step((2, 2 * i), (2, 2 * i + 1))
+
+    teacher_step((0, 2), (1, 2), (3, 2))
 
     for b in planes:
         base = role_at[b] * 16 + div(y_at[b], 4)
 
-        @pl.loop(0, 8, unroll=4)
+        @pl.loop(0, 8, unroll=8)
         def _(i, base=base):
             fill_messages(acc, tl_snd, base + i + 2 * div(i, 2), plain_index)
 
@@ -496,14 +488,14 @@
         def top_step(i, top):
             return jnp.maximum(top, jnp.max(ref[pl.ds(i * 16, 16)].astype(F32), axis=0))
 
-        top = lax.fori_loop(0, 8, top_step, jnp.full((8, 128), -jnp.inf, F32))
+        top = lax.fori_loop(0, 8, top_step, jnp.full((8, 128), -jnp.inf, F32), unroll=4)
         top = over(top, jnp.maximum, jnp.max)
 
         def sum_step(i, total):
             part = jnp.exp(ref[pl.ds(i * 16, 16)].astype(F32) - top[None])
             return total + jnp.sum(part, axis=0)
 
-        total = lax.fori_loop(0, 8, sum_step, jnp.zeros((8, 128), F32))
+        total = lax.fori_loop(0, 8, sum_step, jnp.zeros((8, 128), F32), unroll=4)
         return top + jnp.log(over(total, jnp.add, jnp.sum))
 
     load_order.wait()
@@ -539,7 +531,7 @@
     for b in planes:
         base = role_at[b] * 64 + y_at[b]
         total = lax.fori_loop(
-            0, 32, lambda j, carry, base=base: term(base + j + 8 * div(j, 8), carry), total, unroll=8
+            0, 32, lambda j, carry, base=base: term(base + j + 8 * div(j, 8), carry), total, unroll=16
         )
         send_plane(g_snd, g_rcv, 2, b)
     g_rcv[flat] = g_snd[flat]
@@ -572,7 +564,7 @@
 
     bulk_wait(g_rcv, bulk_r, 2)
 
-    @pl.loop(0, 16)
+    @pl.loop(0, 16, unroll=4)
     def _(g):
         rows = []
         for h in range(2):
@@ -600,7 +592,7 @@
         summed = hb[part] + sib_rcv[part].astype(F32)
         hb[part] = summed
         p1_snd[part] = (summed if axis == Y else jnp.swapaxes(summed, 0, 1)).astype(BF16)
-        for i, d in enumerate(steps):
+        for i, d in enumerate((2, 1, 3)):
             send(p1_snd.at[part, moved(axis, d)], p1_rcv.at[part, i], line(axis, d), "line", part)
 
     g2t[...] = g2_ref[...].astype(F32).T.astype(BF16)

time: 87.8 us -> 85.8 us (0.977)
  Pallas kernels: 85.2 us -> 83.1 us
    pallas_call x1, Pallas kernels: 80.8 us -> 78.7 us  [body(): pl.pallas_call(kernel, out_shape=(jax.ShapeDtypeStruct((1, 1), F32), jax....]
where the time goes in v5:
time: 85.8 us; the launch traced here: 85.6 us
  Pallas kernels  83.1 us (97%)
  between operations  2.45 us (3%)
    pallas_call x1, Pallas kernels, body(): pl.pallas_call(kernel, out_shape=(jax.ShapeDtypeStruct((1, 1), F32), jax....  78.7 us
    pallas_call x1, Pallas kernels, body(): pl.pallas_call(head_kernel, out_shape=(jax.ShapeDtypeStruct((512, 4096),...  4.4 us

profile of v5, /device:TPU:1, one launch (start us, length us, event | category | flops | bytes accessed | tf_op | source)
XLA Modules:
  0.0 85.6 jit_solution(17889712176710589132)
XLA Ops:
  0.6 78.7 %distill.1 = (f32[1,1]{1,0:T(1,128)}, f32[2,4096]{1,0:T(2,128)}, bf16[512,256]{1,0:T(8,128)(2,1)}, bf16[8,16,16,512]{3,2,1,0:T(8,128)(2,1)}) custom-call(bf16[128,256]{1,0:T(8,128)(2,1)} %t_hbm.1, bf16[16384]{0:T(1024)(128)(2,1)} %tg_hbm.1, bf16[512,16384]{1,0:T(8,128)(2,1)} %th_hbm.1, bf16[2,4096]{1,0:T(2,128)(2,1)} %s_hbm.1, bf16[4096]{0:T(1024)(128)(2,1)} %sg_hbm.1, ...), custom_call_target="tpu_custom_call" | custom-call | flops 7516192768 | bytes 25165824 | tf_op jit(solution)/shard_map/distill/pallas_call | solution.py:699
  79.4 4.4 %head.1 = (bf16[512,4096]{1,0:T(8,128)(2,1)}, f32[2,4096]{1,0:T(2,128)}) custom-call(bf16[512,256]{1,0:T(8,128)(2,1)} %get-tuple-element.10.grad_hbm, bf16[8,16,16,512]{3,2,1,0:T(8,128)(2,1)} %get-tuple-element.11.rows_hbm, f32[2,4096]{1,0:T(2,128)} %get-tuple-element.12.ig_hbm), custom_call_target="tpu_custom_call" | custom-call | flops 1073741824 | bytes 6291456 | tf_op jit(solution)/shard_map/head/pallas_call | solution.py:770
